TPU v7x, 128 devices: a whole 4x4x4 slice. The times are simulated.
128 devices in a mesh: chain: 32 (over x, y, core), seq: 4 (over z).
Axes of the slice: x: 4, y: 4, z: 4, core: 2. Of those that a mesh axis runs over, the one named last changes fastest.
Arguments:
- tokens: bfloat16 [32, 3, 512, 768], P('chain', None, 'seq'), may hold values from -6 to 6
- documents: int32 [32, 3, 512], P('chain', None, 'seq'), may hold values from 0 to 4, as said below
- resets: int32 [32, 2], P('chain'), may hold values 0 or 1
- cotangent: bfloat16 [32, 3, 512, 768], P('chain', None, 'seq'), may hold values from -6 to 6
- query_weight: bfloat16 [768, 768], replicated, may hold values from -0.21875 to 0.21875
- query_bias: bfloat16 [768], replicated, may hold values from -1.25 to 1.25
- key_weight: bfloat16 [768, 768], replicated, may hold values from -0.21875 to 0.21875
- value_weight: bfloat16 [768, 768], replicated, may hold values from -0.21875 to 0.21875
- value_bias: bfloat16 [768], replicated, may hold values from -1.25 to 1.25
- mixer_weight: bfloat16 [768, 768], replicated, may hold values from -1.75 to 1.75
- mixer_bias: bfloat16 [768], replicated, may hold values from -1.25 to 1.25
- first_gain: bfloat16 [768], replicated, may hold values from 0.5 to 1.5
- first_shift: bfloat16 [768], replicated, may hold values from -1.25 to 1.25
- inner_weight: bfloat16 [768, 3072], replicated, may hold values from -0.21875 to 0.21875
- inner_bias: bfloat16 [3072], replicated, may hold values from -1.25 to 1.25
- outer_weight: bfloat16 [3072, 768], replicated, may hold values from -0.109375 to 0.109375
- outer_bias: bfloat16 [768], replicated, may hold values from -1.25 to 1.25
- second_gain: bfloat16 [768], replicated, may hold values from 0.5 to 1.5
- second_shift: bfloat16 [768], replicated, may hold values from -1.25 to 1.25
- memory_init: bfloat16 [20, 768], replicated, may hold values from -6 to 6
- write_offset: bfloat16 [20, 768], replicated, may hold values from -3 to 3
Outputs:
- layer_output: bfloat16 [32, 3, 512, 768], P('chain', None, 'seq')
- input_grad: float32 [32, 3, 512, 768], P('chain', None, 'seq')
- query_weight_grad: float32 [768, 768], replicated
- query_bias_grad: float32 [768], replicated
- key_weight_grad: float32 [768, 768], replicated
- value_weight_grad: float32 [768, 768], replicated
- value_bias_grad: float32 [768], replicated
- mixer_weight_grad: float32 [768, 768], replicated
- mixer_bias_grad: float32 [768], replicated
- first_gain_grad: float32 [768], replicated
- first_shift_grad: float32 [768], replicated
- inner_weight_grad: float32 [768, 3072], replicated
- inner_bias_grad: float32 [3072], replicated
- outer_weight_grad: float32 [3072, 768], replicated
- outer_bias_grad: float32 [768], replicated
- second_gain_grad: float32 [768], replicated
- second_shift_grad: float32 [768], replicated
- memory_init_grad: float32 [20, 768], replicated
- write_offset_grad: float32 [20, 768], replicated
- memory_norm: float32 [], replicated
Inputs may be any that keep to these rules, and one draw needn't show every extreme that they name: `documents`: within a segment the ids never fall; a segment's first token has id 0 and its last token id 4.
All inputs are finite; a program needn't handle non-finite values. No bound on the sum of `resets` on one device may be relied on, other than what follows from the above.
Results may differ from a plain program's by a relative error of at most 0.04.
Values may be sent and summed in bfloat16 or wider, within the bound.
A program may use at most 256 MiB of HBM per device.

v0:
```python
import jax
import jax.numpy as jnp
from jax import lax
from jax.sharding import PartitionSpec as P

HEADS = 12


EPS = 1e-12


def shifted(block, axis, distance):
    devices = range(lax.axis_size(axis))
    route = [((i - distance) % len(devices), i) for i in devices]
    return lax.ppermute(block, axis, route)


def layer_norm(hidden, gain, shift):
    centre = hidden - jnp.mean(hidden, axis=-1, keepdims=True)
    spread = jnp.mean(centre * centre, axis=-1, keepdims=True)
    return centre * lax.rsqrt(spread + EPS) * gain + shift


def norm_back(hidden, gain, shift, upstream):
    _, pull = jax.vjp(layer_norm, hidden, gain, shift)
    return pull(upstream)


def gelu_exact(values):
    return jax.nn.gelu(values, approximate=False)


def project(left, right):
    return jnp.dot(left, right, preferred_element_type=jnp.float32)


def back_project(grads, weight):
    return lax.dot_general(
        grads, weight, (((1,), (1,)), ((), ())), preferred_element_type=jnp.float32
    )


def outer_sum(left, right):
    return lax.dot_general(
        left, right, (((0,), (0,)), ((), ())), preferred_element_type=jnp.float32
    )


def column_sum(values):
    return jnp.sum(values.astype(jnp.float32), axis=0)


def split_heads(values):
    return values.reshape(values.shape[0], HEADS, values.shape[1] // HEADS)


def visibility(query_marks, key_marks):
    same = query_marks[:, None] == key_marks[None, :]
    either = (query_marks[:, None] == -1) | (key_marks[None, :] == -1)
    return same | either


def placed(values, start, total_rows):
    empty = jnp.zeros((total_rows, values.shape[1]), jnp.float32)
    return lax.dynamic_update_slice_in_dim(empty, values, start, 0)


def shards(
    tokens,
    documents,
    resets,
    cotangent,
    query_weight,
    query_bias,
    key_weight,
    value_weight,
    value_bias,
    mixer_weight,
    mixer_bias,
    first_gain,
    first_shift,
    inner_weight,
    inner_bias,
    outer_weight,
    outer_bias,
    second_gain,
    second_shift,
    memory_init,
    write_offset,
):
    ranks = lax.axis_size("seq")
    place = lax.axis_index("seq")
    segments = tokens.shape[1]
    block = tokens.shape[2]
    model = tokens.shape[3]
    slots = memory_init.shape[0]
    group = slots // ranks
    width = block + 2 * group
    depth = model // HEADS
    scale = depth ** (-0.5)
    read_start = place * group
    write_start = (place + ranks - 1) % ranks * group
    gain_one = first_gain.astype(jnp.float32)
    shift_one = first_shift.astype(jnp.float32)
    gain_two = second_gain.astype(jnp.float32)
    shift_two = second_shift.astype(jnp.float32)
    init_read = lax.dynamic_slice_in_dim(memory_init, read_start, group, 0)
    init_write = lax.dynamic_slice_in_dim(memory_init, write_start, group, 0)
    offset_rows = lax.dynamic_slice_in_dim(write_offset, write_start, group, 0).astype(jnp.float32)
    all_labels = lax.all_gather(documents[0], "seq", axis=1, tiled=True)
    key_marks = jnp.concatenate(
        [
            all_labels.reshape(segments, ranks, block),
            jnp.full((segments, ranks, 2 * group), -1, jnp.int32),
        ],
        axis=2,
    ).reshape(segments, ranks * width)
    query_marks = jnp.concatenate(
        [documents[0], jnp.full((segments, 2 * group), -1, jnp.int32)], axis=1
    )
    read_memory = init_read
    write_memory = init_write
    written = jnp.zeros((group, model), jnp.float32)
    outputs = []
    saved = []
    for step in range(segments):
        if step > 0:
            flag = resets[0, step - 1] > 0
            last_rows = written.astype(jnp.bfloat16)
            arrived = shifted(last_rows, "seq", -1)
            read_memory = jnp.where(flag, init_read, arrived)
            write_memory = jnp.where(flag, init_write, last_rows)
        write_in = (write_memory.astype(jnp.float32) + offset_rows).astype(jnp.bfloat16)
        rows = jnp.concatenate([tokens[0, step], read_memory, write_in], axis=0)
        visible = visibility(query_marks[step], key_marks[step])
        queries = (project(rows, query_weight) + query_bias).astype(jnp.bfloat16)
        keys = project(rows, key_weight).astype(jnp.bfloat16)
        values = (project(rows, value_weight) + value_bias).astype(jnp.bfloat16)
        all_keys, all_values = (
            lax.all_gather(keys, "seq", axis=0, tiled=True),
            lax.all_gather(values, "seq", axis=0, tiled=True),
        )
        scores = (
            jnp.einsum(
                "rhd,khd->hrk",
                split_heads(queries),
                split_heads(all_keys),
                preferred_element_type=jnp.float32,
            )
            * scale
        )
        masked = jnp.where(visible[None], scores, -jnp.inf)
        peak = jnp.max(masked, axis=-1, keepdims=True)
        weights = jnp.exp(masked - peak)
        total = jnp.sum(weights, axis=-1, keepdims=True)
        probs = weights / total
        log_total = peak + jnp.log(total)
        mixed = (
            jnp.einsum(
                "hrk,khd->rhd",
                probs.astype(jnp.bfloat16),
                split_heads(all_values),
                preferred_element_type=jnp.float32,
            )
            .reshape(width, model)
            .astype(jnp.bfloat16)
        )
        upper_in = rows.astype(jnp.float32) + project(mixed, mixer_weight) + mixer_bias
        upper = layer_norm(upper_in, gain_one, shift_one)
        upper_low = upper.astype(jnp.bfloat16)
        inner = project(upper_low, inner_weight) + inner_bias
        activated = gelu_exact(inner).astype(jnp.bfloat16)
        result_in = upper + project(activated, outer_weight) + outer_bias
        result = layer_norm(result_in, gain_two, shift_two)
        outputs.append(result[:block].astype(jnp.bfloat16))
        written = result[block + group :]
        saved.append(
            (
                rows,
                visible,
                queries,
                all_keys,
                all_values,
                log_total,
                mixed,
                upper_in,
                upper_low,
                inner,
                activated,
                result_in,
            )
        )
    totals = {}
    for name, shape in (
        ("query_w", (model, model)),
        ("query_b", (model,)),
        ("key_w", (model, model)),
        ("value_w", (model, model)),
        ("value_b", (model,)),
        ("mixer_w", (model, model)),
        ("mixer_b", (model,)),
        ("gain_one", (model,)),
        ("shift_one", (model,)),
        ("inner_w", inner_weight.shape),
        ("inner_b", inner_bias.shape),
        ("outer_w", outer_weight.shape),
        ("outer_b", (model,)),
        ("gain_two", (model,)),
        ("shift_two", (model,)),
        ("init", (slots, model)),
        ("offset", (slots, model)),
    ):
        totals[name] = jnp.zeros(shape, jnp.float32)
    norm_total = jnp.zeros((), jnp.float32)
    carried = jnp.zeros((group, model), jnp.float32)
    input_grads = [None] * segments
    for step in reversed(range(segments)):
        (
            rows,
            visible,
            queries,
            all_keys,
            all_values,
            log_total,
            mixed,
            upper_in,
            upper_low,
            inner,
            activated,
            result_in,
        ) = saved[step]
        upstream = jnp.concatenate(
            [
                cotangent[0, step].astype(jnp.float32),
                jnp.zeros((group, model), jnp.float32),
                carried,
            ],
            axis=0,
        )
        d_result, d_gain_two, d_shift_two = norm_back(result_in, gain_two, shift_two, upstream)
        totals["gain_two"] = totals["gain_two"] + d_gain_two
        totals["shift_two"] = totals["shift_two"] + d_shift_two
        outer_low = d_result.astype(jnp.bfloat16)
        totals["outer_w"] = totals["outer_w"] + outer_sum(activated, outer_low)
        totals["outer_b"] = totals["outer_b"] + column_sum(outer_low)
        d_activated = back_project(outer_low, outer_weight)
        _, gelu_pull = jax.vjp(gelu_exact, inner)
        d_inner = gelu_pull(d_activated)[0].astype(jnp.bfloat16)
        totals["inner_w"] = totals["inner_w"] + outer_sum(upper_low, d_inner)
        totals["inner_b"] = totals["inner_b"] + column_sum(d_inner)
        d_upper = back_project(d_inner, inner_weight) + d_result
        d_upper_in, d_gain_one, d_shift_one = norm_back(upper_in, gain_one, shift_one, d_upper)
        totals["gain_one"] = totals["gain_one"] + d_gain_one
        totals["shift_one"] = totals["shift_one"] + d_shift_one
        branch_low = d_upper_in.astype(jnp.bfloat16)
        totals["mixer_w"] = totals["mixer_w"] + outer_sum(mixed, branch_low)
        totals["mixer_b"] = totals["mixer_b"] + column_sum(branch_low)
        d_mixed_flat = back_project(branch_low, mixer_weight).astype(jnp.bfloat16)
        d_mixed = split_heads(d_mixed_flat)
        query_heads = split_heads(queries)
        key_heads = split_heads(all_keys)
        scores = (
            jnp.einsum("rhd,khd->hrk", query_heads, key_heads, preferred_element_type=jnp.float32)
            * scale
        )
        probs = jnp.where(visible[None], jnp.exp(scores - log_total), 0.0)
        d_probs = jnp.einsum(
            "rhd,khd->hrk", d_mixed, split_heads(all_values), preferred_element_type=jnp.float32
        )
        inner_prod = jnp.sum(probs * d_probs, axis=-1, keepdims=True)
        d_scores = (probs * (d_probs - inner_prod)).astype(jnp.bfloat16)
        d_queries = (
            (
                jnp.einsum("hrk,khd->rhd", d_scores, key_heads, preferred_element_type=jnp.float32)
                * scale
            )
            .reshape(width, model)
            .astype(jnp.bfloat16)
        )
        key_part = (
            jnp.einsum("hrk,rhd->khd", d_scores, query_heads, preferred_element_type=jnp.float32)
            * scale
        ).reshape(ranks * width, model)
        value_part = jnp.einsum(
            "hrk,rhd->khd", probs.astype(jnp.bfloat16), d_mixed, preferred_element_type=jnp.float32
        ).reshape(ranks * width, model)
        d_keys, d_values = (
            lax.psum_scatter(
                key_part.astype(jnp.bfloat16), "seq", scatter_dimension=0, tiled=True
            ).astype(jnp.float32),
            lax.psum_scatter(
                value_part.astype(jnp.bfloat16), "seq", scatter_dimension=0, tiled=True
            ).astype(jnp.float32),
        )
        d_keys = d_keys.astype(jnp.bfloat16)
        d_values = d_values.astype(jnp.bfloat16)
        totals["query_w"] = totals["query_w"] + outer_sum(rows, d_queries)
        totals["query_b"] = totals["query_b"] + column_sum(d_queries)
        totals["key_w"] = totals["key_w"] + outer_sum(rows, d_keys)
        totals["value_w"] = totals["value_w"] + outer_sum(rows, d_values)
        totals["value_b"] = totals["value_b"] + column_sum(d_values)
        d_rows = (
            back_project(d_queries, query_weight)
            + back_project(d_keys, key_weight)
            + back_project(d_values, value_weight)
            + d_upper_in
        )
        input_grads[step] = d_rows[:block]
        read_grad = d_rows[block : block + group]
        write_grad = d_rows[block + group :]
        arrived_grad = shifted(read_grad, "seq", 1)
        memory_grad = arrived_grad + write_grad
        totals["offset"] = totals["offset"] + placed(write_grad, write_start, slots)
        norm_total = norm_total + jnp.sum(memory_grad * memory_grad)
        if step > 0:
            flag = resets[0, step - 1] > 0
            totals["init"] = totals["init"] + placed(
                jnp.where(flag, memory_grad, 0.0), write_start, slots
            )
            carried = jnp.where(flag, 0.0, memory_grad)
        else:
            totals["init"] = totals["init"] + placed(memory_grad, write_start, slots)
    (
        query_w,
        query_b,
        key_w,
        value_w,
        value_b,
        mixer_w,
        mixer_b,
        gain_one_sum,
        shift_one_sum,
        inner_w,
        inner_b,
        outer_w,
        outer_b,
        gain_two_sum,
        shift_two_sum,
        init_sum,
        offset_sum,
        norm_sum,
    ) = lax.psum(
        (
            totals["query_w"],
            totals["query_b"],
            totals["key_w"],
            totals["value_w"],
            totals["value_b"],
            totals["mixer_w"],
            totals["mixer_b"],
            totals["gain_one"],
            totals["shift_one"],
            totals["inner_w"],
            totals["inner_b"],
            totals["outer_w"],
            totals["outer_b"],
            totals["gain_two"],
            totals["shift_two"],
            totals["init"],
            totals["offset"],
            norm_total,
        ),
        ("chain", "seq"),
    )
    memory_norm = jnp.sqrt(norm_sum / (lax.axis_size("chain") * segments * slots * model))
    layer_output = jnp.stack(outputs)[None]
    input_grad = jnp.stack(input_grads)[None]
    return (
        layer_output,
        input_grad,
        query_w,
        query_b,
        key_w,
        value_w,
        value_b,
        mixer_w,
        mixer_b,
        gain_one_sum,
        shift_one_sum,
        inner_w,
        inner_b,
        outer_w,
        outer_b,
        gain_two_sum,
        shift_two_sum,
        init_sum,
        offset_sum,
        memory_norm,
    )


def solution(mesh):
    in_specs = (
        P("chain", None, "seq", None),
        P("chain", None, "seq"),
        P("chain", None),
        P("chain", None, "seq", None),
        P(),
        P(),
        P(),
        P(),
        P(),
        P(),
        P(),
        P(),
        P(),
        P(),
        P(),
        P(),
        P(),
        P(),
        P(),
        P(),
        P(),
    )
    out_specs = (
        P("chain", None, "seq", None),
        P("chain", None, "seq", None),
        P(),
        P(),
        P(),
        P(),
        P(),
        P(),
        P(),
        P(),
        P(),
        P(),
        P(),
        P(),
        P(),
        P(),
        P(),
        P(),
        P(),
        P(),
    )
    return jax.shard_map(shards, mesh=mesh, in_specs=in_specs, out_specs=out_specs, check_vma=False)
```

profile of v0, /device:TPU:1, one launch (start us, length us, event | category | flops | bytes accessed | tf_op | source)
XLA Modules:
  0.0 814.0 jit_solution(16803241573845840343)
XLA Ops:
  8.0 10.1 %all-gather = s32[1,3,512]{2,0,1:T(1,128)S(1)} all-gather(s32[1,3,128]{2,0,1:T(1,128)} %param.22), channel_id=2, replica_groups=mesh['chain'=32,'seq'=4] {'seq'}, dimensions={2}, use_global_device_ids=true | all-gather | bytes 7680 | tf_op jit(solution)/shard_map/all_gather | solution.py:110
  38.8 11.7 %all-gather.2 = bf16[4,138,768]{2,1,0:T(8,128)(2,1)S(1)} all-gather(bf16[1,138,768]{2,1,0:T(8,128)(2,1)S(1)} %fusion.73), channel_id=1, replica_groups=mesh['chain'=32,'seq'=4] {'seq'}, dimensions={0}, use_global_device_ids=true | all-gather | bytes 1059840 | tf_op jit(solution)/shard_map/all_gather | solution.py:140
  50.8 11.8 %all-gather.1 = bf16[4,138,768]{2,1,0:T(8,128)(2,1)} all-gather(bf16[1,138,768]{2,1,0:T(8,128)(2,1)S(1)} %fusion.78), channel_id=1, replica_groups=mesh['chain'=32,'seq'=4] {'seq'}, dimensions={0}, use_global_device_ids=true | all-gather | bytes 1059840 | tf_op jit(solution)/shard_map/all_gather | solution.py:141
  83.2 7.1 multiply_convert_fusion.8
  93.1 13.0 %collective-permute-start = (bf16[5,768]{1,0:T(8,128)(2,1)}, bf16[5,768]{1,0:T(8,128)(2,1)}, u32[]{:S(2)}, u32[]{:S(2)}) collective-permute-start(bf16[5,768]{1,0:T(8,128)(2,1)} %slice.123), channel_id=1, source_target_pairs={{1,0},{2,1},{3,2},{0,3},{5,4},{6,5},{7,6},{4,7},{9,8},{10,9},{11,1... | collective-permute-start | bytes 23048 | tf_op jit(solution)/shard_map/ppermute | solution.py:15
  126.3 13.0 %all-gather.4 = bf16[4,138,768]{2,1,0:T(8,128)(2,1)} all-gather(bf16[1,138,768]{2,1,0:T(8,128)(2,1)} %fusion.74), channel_id=1, replica_groups=mesh['chain'=32,'seq'=4] {'seq'}, dimensions={0}, use_global_device_ids=true | all-gather | bytes 1059840 | tf_op jit(solution)/shard_map/all_gather | solution.py:140
  139.3 14.5 %all-gather.3 = bf16[4,138,768]{2,1,0:T(8,128)(2,1)} all-gather(bf16[1,138,768]{2,1,0:T(8,128)(2,1)} %fusion.77), channel_id=1, replica_groups=mesh['chain'=32,'seq'=4] {'seq'}, dimensions={0}, use_global_device_ids=true | all-gather | bytes 1059840 | tf_op jit(solution)/shard_map/all_gather | solution.py:141
  157.3 3.9 reshape.581
  176.3 7.1 multiply_convert_fusion.7
  190.3 11.4 %all-gather.6 = bf16[4,138,768]{2,1,0:T(8,128)(2,1)} all-gather(bf16[1,138,768]{2,1,0:T(8,128)(2,1)S(1)} %fusion.75), channel_id=1, replica_groups=mesh['chain'=32,'seq'=4] {'seq'}, dimensions={0}, use_global_device_ids=true | all-gather | bytes 1059840 | tf_op jit(solution)/shard_map/all_gather | solution.py:140
  201.7 13.1 %all-gather.5 = bf16[4,138,768]{2,1,0:T(8,128)(2,1)} all-gather(bf16[1,138,768]{2,1,0:T(8,128)(2,1)S(1)} %copy-done.111), channel_id=1, replica_groups=mesh['chain'=32,'seq'=4] {'seq'}, dimensions={0}, use_global_device_ids=true | all-gather | bytes 1059840 | tf_op jit(solution)/shard_map/all_gather | solution.py:141
  233.1 4.6 multiply_convert_fusion.6
  249.0 4.5 fusion.51
  253.5 4.3 multiply_reduce_fusion.2
  266.7 5.1 fusion.173
  271.9 5.3 fusion.140
  277.1 60.0 %all-reduce.26.cloned.1.call-done = (bf16[552,768]{0,1:T(8,128)(2,1)}, bf16[552,768]{0,1:T(8,128)(2,1)}) async-done(((bf16[552,768]{0,1:T(8,128)(2,1)}, bf16[552,768]{0,1:T(8,128)(2,1)}), (bf16[552,768]{0,1:T(8,128)(2,1)}, bf16[552,768]{0,1:T(8,128)(2,1)})) %all-reduce.26.cloned.1.call-update) | async-done | bytes 1695760
  348.7 4.9 convert_reduce_fusion.1
  360.9 4.7 fusion.48
  365.6 4.1 multiply_reduce_fusion.1
  385.8 5.0 fusion.174
  390.8 5.3 fusion.143
  396.1 36.1 %all-reduce.24.cloned.1.call-done = (bf16[552,768]{0,1:T(8,128)(2,1)}, bf16[552,768]{0,1:T(8,128)(2,1)}) async-done(((bf16[552,768]{0,1:T(8,128)(2,1)}, bf16[552,768]{0,1:T(8,128)(2,1)}), (bf16[552,768]{0,1:T(8,128)(2,1)}, bf16[552,768]{0,1:T(8,128)(2,1)})) %all-reduce.24.cloned.1.call-update) | async-done | bytes 1695760
  456.6 4.7 fusion.45
  461.3 4.1 multiply_reduce_fusion
  475.0 4.7 add_add_fusion.5
  479.8 12.9 %add_add_fusion = f32[3072,768]{1,0:T(8,128)} fusion(f32[3072,768]{1,0:T(8,128)} %fusion.173, f32[3072,768]{1,0:T(8,128)} %fusion.174, bf16[138,3072]{1,0:T(8,128)(2,1)} %copy-done.50, bf16[138,768]{1,0:T(8,128)(2,1)} %copy-done.96), kind=kOutput, calls=%fused_computation | convolution fusion | flops 655884288 | bytes 29371392 | tf_op jit(solution)/shard_map/dot_general | solution.py:44
  492.8 5.3 add_add_fusion.1
  498.0 33.8 %all-reduce.22.cloned.1.call-done = (bf16[552,768]{0,1:T(8,128)(2,1)}, bf16[552,768]{0,1:T(8,128)(2,1)}) async-done(((bf16[552,768]{0,1:T(8,128)(2,1)}, bf16[552,768]{0,1:T(8,128)(2,1)}), (bf16[552,768]{0,1:T(8,128)(2,1)}, bf16[552,768]{0,1:T(8,128)(2,1)})) %all-reduce.22.cloned.1.call-update) | async-done | bytes 1695760
  563.3 69.1 %all-reduce.27 = (f32[768]{0:T(1024)}, f32[768]{0:T(1024)}, f32[768]{0:T(1024)}, f32[768]{0:T(1024)}, f32[768]{0:T(1024)}, /*index=5*/f32[3072]{0:T(1024)}, f32[...) all-reduce(f32[768]{0:T(1024)S(1)} %add.566, ...), channel_id=1, replica_groups=mesh['chain'=32,'seq'=4] {'chain','seq'}, use_global_device_ids=true, to_apply=%region_43.44 | all-reduce | flops 39937 | bytes 319496 | tf_op jit(solution)/shard_map/psum | solution.py:342
  633.1 150.1 %all-reduce.20.cloned.1.call-done = (f32[768,768]{1,0:T(8,128)}, f32[768,768]{1,0:T(8,128)}, f32[768,768]{1,0:T(8,128)}, f32[768,768]{1,0:T(8,128)}, f32[768,3072]{1,0:T(8,128)}, /*index=5*/f32[3072,768]{1,0:T(8,128)}) async-done(((f32[768,768]{1,0:T(8,128)}, f32[768,768]{1,0:T(8,128)}, f32[768,768]{1,0:T(8,128)}, f32[768,768]{1,0:T(8,128)}, f32[768,3072]{1,0:T(8,128)}, /*index=5*/f32[3072,768]{1,0:T(8,128)}), ...) | async-done | bytes 28311568 | tf_op jit(solution)/shard_map/psum | solution.py:342
  793.0 9.3 %copy.138 = f32[768,3072]{1,0:T(8,128)} copy(f32[768,3072]{1,0:T(8,128)} %get-tuple-element.189) | data formatting | bytes 18874368
  (761 shorter events, 236.3 us)
Async XLA Ops:
  7.2 74.5 %copy-start = (bf16[768,768]{1,0:T(8,128)(2,1)S(1)}, bf16[768,768]{1,0:T(8,128)(2,1)}, u32[]{:S(2)}) copy-start(bf16[768,768]{1,0:T(8,128)(2,1)} %param.30) | copy-start | bytes 3538948
  7.2 329.9 %all-reduce.26.cloned.1.call-start = ((), (), s32[]{:S(2)}) async-start(), calls=%async_computation.3 | async-start | bytes 3932160
  35.4 15.0 %copy-start.14 = (bf16[768,768]{1,0:T(8,128)(2,1)S(1)}, bf16[768,768]{1,0:T(8,128)(2,1)}, u32[]{:S(2)}) copy-start(bf16[768,768]{1,0:T(8,128)(2,1)} %param.28) | copy-start | bytes 3538948
  37.4 13.0 %copy-start.223 = (f32[768]{0:T(1024)S(1)}, f32[768]{0:T(1024)}, u32[]{:S(2)}) copy-start(f32[768]{0:T(1024)} %convert_element_type.377) | copy-start | bytes 9220
  90.3 16.3 %copy-start.225 = (s32[1,2]{1,0:T(1,128)S(1)}, s32[1,2]{1,0:T(1,128)}, u32[]{:S(2)}) copy-start(s32[1,2]{1,0:T(1,128)} %param.23) | copy-start | bytes 28
  90.4 16.9 %copy-start.213 = (s32[1,138]{1,0:T(1,128)S(1)}, s32[1,138]{1,0:T(1,128)}, u32[]{:S(2)}) copy-start(s32[1,138]{1,0:T(1,128)} %get-tuple-element.134) | copy-start | bytes 1660
  90.4 17.4 %copy-start.212 = (s32[1,138]{1,0:T(1,128)S(1)}, s32[1,138]{1,0:T(1,128)}, u32[]{:S(2)}) copy-start(s32[1,138]{1,0:T(1,128)} %get-tuple-element.133) | copy-start | bytes 1660
  90.4 17.9 %copy-start.184 = (s32[1,4,138]{2,1,0:T(4,128)S(1)}, s32[1,4,138]{2,1,0:T(4,128)}, u32[]{:S(2)}) copy-start(s32[1,4,138]{2,1,0:T(4,128)} %get-tuple-element.130) | copy-start | bytes 6628
  90.4 18.5 %copy-start.183 = (s32[1,4,138]{2,1,0:T(4,128)S(1)}, s32[1,4,138]{2,1,0:T(4,128)}, u32[]{:S(2)}) copy-start(s32[1,4,138]{2,1,0:T(4,128)} %get-tuple-element.131) | copy-start | bytes 6628
  91.4 17.5 %copy-start.164 = (f32[138]{0:T(256)}, f32[138]{0:T(256)S(1)}, u32[]{:S(2)}) copy-start(f32[138]{0:T(256)S(1)} %broadcast_multiply_fusion.4) | copy-start | bytes 1660
  91.7 17.3 %copy-start.206 = (f32[138]{0:T(256)}, f32[138]{0:T(256)S(1)}, u32[]{:S(2)}) copy-start(f32[138]{0:T(256)S(1)} %multiply_reduce_fusion.17) | copy-start | bytes 1660
  92.2 16.8 %copy-start.185 = (f32[138]{0:T(256)}, f32[138]{0:T(256)S(1)}, u32[]{:S(2)}) copy-start(f32[138]{0:T(256)S(1)} %fusion.123) | copy-start | bytes 1660
  92.4 16.6 %copy-start.99 = (bf16[138,768]{1,0:T(8,128)(2,1)}, bf16[138,768]{1,0:T(8,128)(2,1)S(1)}, u32[]{:S(2)}) copy-start(bf16[138,768]{1,0:T(8,128)(2,1)S(1)} %add_convert_fusion.4) | copy-start | bytes 635908
  93.1 26.3 %collective-permute-start = (bf16[5,768]{1,0:T(8,128)(2,1)}, bf16[5,768]{1,0:T(8,128)(2,1)}, u32[]{:S(2)}, u32[]{:S(2)}) collective-permute-start(bf16[5,768]{1,0:T(8,128)(2,1)} %slice.123), channel_id=1, source_target_pairs={{1,0},{2,1},{3,2},{0,3},{5,4},{6,5},{7,6},{4,7},{9,8},{10,9},{11,1... | collective-permute-start | bytes 23048 | tf_op jit(solution)/shard_map/ppermute | solution.py:15
  185.6 2.6 collective-permute-start.1
  190.3 35.4 %copy-start.48 = (bf16[138,768]{0,1:T(8,128)(2,1)}, bf16[138,768]{0,1:T(8,128)(2,1)S(1)}, u32[]{:S(2)}) copy-start(bf16[138,768]{0,1:T(8,128)(2,1)S(1)} %copy.84) | copy-start | bytes 635908
  230.2 23.4 %copy-start.135 = (f32[12,138]{1,0:T(8,128)}, f32[12,138]{1,0:T(8,128)S(1)}, u32[]{:S(2)}) copy-start(f32[12,138]{1,0:T(8,128)S(1)} %log_add_fusion) | copy-start | bytes 19876
  232.8 13.7 %copy-start.6 = (f32[138,768]{1,0:T(8,128)}, f32[138,768]{1,0:T(8,128)S(1)}, u32[]{:S(2)}) copy-start(f32[138,768]{1,0:T(8,128)S(1)} %get-tuple-element.101) | copy-start | bytes 1271812
  232.8 13.6 %copy-start.147 = (f32[138]{0:T(256)}, f32[138]{0:T(256)S(1)}, u32[]{:S(2)}) copy-start(f32[138]{0:T(256)S(1)} %broadcast_multiply_fusion.1) | copy-start | bytes 1660
  233.1 13.4 %copy-start.159 = (f32[138]{0:T(256)}, f32[138]{0:T(256)S(1)}, u32[]{:S(2)}) copy-start(f32[138]{0:T(256)S(1)} %fusion.126) | copy-start | bytes 1660
  261.7 170.6 %all-reduce.24.cloned.1.call-start = ((), (), s32[]{:S(2)}) async-start(), calls=%async_computation.2 | async-start | bytes 3932160
  277.1 62.2 %copy-start.15 = (bf16[768,768]{1,0:T(8,128)(2,1)S(1)}, bf16[768,768]{1,0:T(8,128)(2,1)}, u32[]{:S(2)}) copy-start(bf16[768,768]{1,0:T(8,128)(2,1)} %param.28) | copy-start | bytes 3538948
  277.1 62.2 %copy-start.35 = (f32[138,768]{1,0:T(8,128)S(1)}, f32[138,768]{1,0:T(8,128)}, u32[]{:S(2)}) copy-start(f32[138,768]{1,0:T(8,128)} %copy-done.34) | copy-start | bytes 1271812
  341.4 4.2 collective-permute-start.2
  375.2 156.6 %all-reduce.22.cloned.1.call-start = ((), (), s32[]{:S(2)}) async-start(), calls=%async_computation.1 | async-start | bytes 3932160
  396.1 39.5 %copy-start.87 = (f32[138,768]{1,0:T(8,128)S(1)}, f32[138,768]{1,0:T(8,128)}, u32[]{:S(2)}) copy-start(f32[138,768]{1,0:T(8,128)} %fusion.169) | copy-start | bytes 1271812
  432.2 14.5 %slice-start.18 = ((s8[4718592]{0:T(1024)(128)(4,1)}), s8[4194304]{0:T(1024)(128)(4,1)S(1)}, s32[]{:S(2)}) async-start(s8[4718592]{0:T(1024)(128)(4,1)} %bitcast.234), calls=%async_computation.22 | async-start | bytes 8388608
  438.4 4.4 collective-permute-start.3
  474.8 308.4 %all-reduce.20.cloned.1.call-start = ((), (), s32[]{:S(2)}) async-start(), calls=%async_computation | async-start | bytes 56623104 | tf_op jit(solution)/shard_map/psum | solution.py:342
  475.0 17.7 %slice-start.6 = ((s8[9437184]{0:T(1024)(128)(4,1)}), s8[4194304]{0:T(1024)(128)(4,1)S(1)}, s32[]{:S(2)}) async-start(s8[9437184]{0:T(1024)(128)(4,1)} %bitcast.224), calls=%async_computation.10 | async-start | bytes 8388608
  475.0 17.7 %slice-start.9 = ((s8[9437184]{0:T(1024)(128)(4,1)}), s8[4194304]{0:T(1024)(128)(4,1)S(1)}, s32[]{:S(2)}) async-start(s8[9437184]{0:T(1024)(128)(4,1)} %bitcast.226), calls=%async_computation.13 | async-start | bytes 8388608
  557.0 4.5 collective-permute-start.4
  (241 other events, 1138.1 us)
Sparse Core Ops, SparseCore 0:
  261.8 75.2 all-reduce.25
  375.3 56.8 all-reduce.23
  474.9 56.8 all-reduce.21
  542.3 240.8 all-reduce.19
where the time goes:
time: 819 us; the launch traced here: 814 us
  waiting for transfers between devices  288 us (35%)
  matrix products  188 us (23%)
  blocking collectives  155 us (19%)
  local copies, waits for them, and re-layouts  93.6 us (11%)
  other arithmetic  51.3 us (6%)
  between operations  23.1 us (3%)
  starting transfers between devices  15.1 us (2%)
    psum x1, waiting for transfers between devices, shards(): lax.psum((totals['query_w'], totals['query_b'], totals['key_w'], totals['...  150 us
    unnamed x7, waiting for transfers between devices  130 us
    dot_general x18, matrix products, outer_sum(): lax.dot_general(left, right, (((0,), (0,)), ((), ())), preferred_element_...  70 us
    psum x1, blocking collectives, shards(): lax.psum((totals['query_w'], totals['query_b'], totals['key_w'], totals['...  69.1 us
    all_gather x3, blocking collectives, shards(): lax.all_gather(values, 'seq', axis=0, tiled=True)  39.4 us
    unnamed x536, local copies, waits for them, and re-layouts  36.9 us
    all_gather x3, blocking collectives, shards(): lax.all_gather(keys, 'seq', axis=0, tiled=True)  36 us
    dot_general x18, matrix products, back_project(): lax.dot_general(grads, weight, (((1,), (1,)), ((), ())), preferred_elemen...  35.1 us
  transfers between devices with their start and end apart: 9, of which 8 were waited for; matrix products, arithmetic and copies ran while one was open for 11% of the time, Pallas kernels for 0%

commit v1 on v0

v1 whole, which is shorter than its diff:
```python
import functools

import jax
import jax.numpy as jnp
from jax import lax
from jax.experimental import pallas as pl
from jax.experimental.pallas import tpu as pltpu
from jax.sharding import PartitionSpec as P

MESH = pl.DeviceIdType.MESH
LOW = jnp.bfloat16
F32 = jnp.float32
SEGS = 3
BLOCK = 128
MODEL = 768
INNER = 3072
SLOTS = 20
PAD = 32
MEMORY = 2 * PAD
ROWS = SEGS * BLOCK
TOKENS = 512
KEYS = 640
QUERIES = TOKENS + PAD
HEAD = 64
MINE = 3
GROUP = MINE * HEAD
TRIPLE = 3 * GROUP
SCALE = HEAD ** (-0.5)
EPS = 1e-12
HIDDEN = -1e30


def dot(left, right):
    return jnp.dot(left, right, preferred_element_type=F32)


def dot_t(left, right):
    return lax.dot_general(left, right, (((1,), (1,)), ((), ())), preferred_element_type=F32)


def t_dot(left, right):
    return lax.dot_general(left, right, (((0,), (0,)), ((), ())), preferred_element_type=F32)


def norm_parts(hidden):
    centre = hidden - jnp.mean(hidden, axis=-1, keepdims=True)
    spread = jnp.mean(centre * centre, axis=-1, keepdims=True)
    inverse = lax.rsqrt(spread + EPS)
    return centre * inverse, inverse


def norm_back(upstream, unit, inverse, gain):
    scaled = upstream * gain
    first = jnp.mean(scaled, axis=-1, keepdims=True)
    second = jnp.mean(scaled * unit, axis=-1, keepdims=True)
    return (scaled - first - unit * second) * inverse


def gelu_parts(values):
    below = 0.5 * (1.0 + lax.erf(values * (0.5**0.5)))
    density = jnp.exp(-0.5 * values * values) * 0.3989422804014327
    return values * below, below + values * density


def column_sum(values):
    return jnp.sum(values.astype(F32), axis=0, keepdims=True)


def ring(off):
    return lax.rem(lax.axis_index("seq") + off + 4, 4)


def ring_barrier():
    barrier = pltpu.get_barrier_semaphore()
    for off in (1, 2, 3):
        pl.semaphore_signal(
            barrier, inc=1, device_id=(lax.axis_index("chain"), ring(off)), device_id_type=MESH
        )
    pl.semaphore_wait(barrier, 3)


def push(started, src, dst, s_sem, r_sem, off):
    copy = pltpu.make_async_remote_copy(
        src_ref=src,
        dst_ref=dst,
        send_sem=s_sem,
        recv_sem=r_sem,
        device_id=(lax.axis_index("chain"), ring(off)),
        device_id_type=MESH,
    )
    copy.start()
    started.append(copy)
    return copy


def fetch(pairs, sems):
    copies = [pltpu.make_async_copy(src, dst, sems.at[i]) for i, (src, dst) in enumerate(pairs)]
    for copy in copies:
        copy.start()
    return copies


QUERY_B, VALUE_B, MIXER_B, GAIN_1, SHIFT_1, OUTER_B, GAIN_2, SHIFT_2 = range(8)


def forward_kernel(
    resets, tok, docs, init, offset, vec, inner_b,
    wq_h, wk_h, wv_h, wm_h, wi_h, wo_h,
    kv, probs, orow, ow, h1w, zw, h2w, xm,
    wq, wk, wv, wm, wi, wo, wown, vown, sbuf, lab, bias, osend, owsend,
    w_sem, q_s, q_r, o_s, o_r, m_s, m_r, l_s, l_r,
):
    z = lax.axis_index("seq")
    fetched = fetch(
        [(wq_h, wq), (wk_h, wk), (wv_h, wv), (wm_h, wm), (wi_h, wi), (wo_h, wo)], w_sem
    )
    started = []
    ring_barrier()
    lab[pl.ds(z, 1)] = docs[...][None]
    label_copies = [
        push(started, docs, lab.at[z], l_s.at[d - 1], l_r.at[d - 1], d) for d in (1, 2, 3)
    ]
    tokens = tok[...].reshape(ROWS, MODEL)
    fetched[0].wait()
    queries = ((dot(tokens, wq[...]) + vec[QUERY_B : QUERY_B + 1, :]) * SCALE).astype(LOW)
    for g in range(4):
        for s in range(SEGS):
            sbuf[g, s, :, 0:GROUP] = queries[
                s * BLOCK : (s + 1) * BLOCK, g * GROUP : (g + 1) * GROUP
            ]
    fetched[1].wait()
    keys = dot(tokens, wk[...]).astype(LOW)
    for g in range(4):
        for s in range(SEGS):
            sbuf[g, s, :, GROUP : 2 * GROUP] = keys[
                s * BLOCK : (s + 1) * BLOCK, g * GROUP : (g + 1) * GROUP
            ]
    fetched[2].wait()
    values = (dot(tokens, wv[...]) + vec[VALUE_B : VALUE_B + 1, :]).astype(LOW)
    for g in range(4):
        for s in range(SEGS):
            sbuf[g, s, :, 2 * GROUP :] = values[
                s * BLOCK : (s + 1) * BLOCK, g * GROUP : (g + 1) * GROUP
            ]
    here = pl.ds(pl.multiple_of(z * BLOCK, BLOCK), BLOCK)
    row_copies = []
    for s in range(SEGS):
        row_copies.append(
            [
                push(
                    started, sbuf.at[ring(d), s], kv.at[s, here],
                    q_s.at[s, d - 1], q_r.at[s, d - 1], d,
                )
                for d in (1, 2, 3)
            ]
        )
    for s in range(SEGS):
        kv[s, here, :] = sbuf[z, s]
        kv[s, TOKENS + MEMORY :, :] = jnp.zeros((KEYS - TOKENS - MEMORY, TRIPLE), LOW)
    for g in range(4):

        @pl.when(z == g)
        def _():
            cut = slice(g * GROUP, (g + 1) * GROUP)
            wown[:, 0:GROUP] = wq[:, cut]
            wown[:, GROUP : 2 * GROUP] = wk[:, cut]
            wown[:, 2 * GROUP :] = wv[:, cut]
            vown[0:1, 0:GROUP] = vec[QUERY_B : QUERY_B + 1, cut]
            vown[0:1, GROUP : 2 * GROUP] = jnp.zeros((1, GROUP), F32)
            vown[0:1, 2 * GROUP :] = vec[VALUE_B : VALUE_B + 1, cut]

    lane = lax.broadcasted_iota(jnp.int32, (1, TRIPLE), 1)
    factor = jnp.where(lane < GROUP, SCALE, 1.0)
    slot = lax.broadcasted_iota(jnp.int32, (PAD, MODEL), 0)
    key_lane = lax.broadcasted_iota(jnp.int32, (PAD, KEYS), 1)
    filled = (key_lane < TOKENS + SLOTS) | (
        (key_lane >= TOKENS + PAD) & (key_lane < TOKENS + PAD + SLOTS)
    )
    write_bias = jnp.where(filled, 0.0, HIDDEN)

    def attend(query_rows, mask, s, row_at, rows):
        parts = []
        for h in range(MINE):
            key_head = kv[s, :, GROUP + h * HEAD : GROUP + (h + 1) * HEAD]
            value_head = kv[s, :, 2 * GROUP + h * HEAD : 2 * GROUP + (h + 1) * HEAD]
            scores = dot_t(query_rows[:, h * HEAD : (h + 1) * HEAD], key_head) + mask
            weights = jnp.exp(scores - jnp.max(scores, axis=-1, keepdims=True))
            total = jnp.sum(weights, axis=-1, keepdims=True)
            prob = (weights * (1.0 / total)).astype(LOW)
            probs[s, h, pl.ds(row_at, rows), :] = prob
            parts.append(dot(prob, value_head))
        return jnp.concatenate(parts, axis=1).astype(LOW)

    memory = init[...]
    for copy in label_copies:
        copy.wait_recv()
    out_copies = []
    for s in range(SEGS):
        written_in = (memory.astype(F32) + offset[...].astype(F32)).astype(LOW)
        xm[s, 0:PAD, :] = written_in
        xm[s, PAD:, :] = memory
        kv[s, TOKENS : TOKENS + MEMORY, :] = (
            (dot(xm[s], wown[...]) + vown[0:1, :]) * factor
        ).astype(LOW)
        for i in range(4):
            column = jnp.transpose(jnp.broadcast_to(lab[i, s : s + 1, :].astype(F32), (BLOCK, BLOCK)))
            for j in range(4):
                row = jnp.broadcast_to(lab[j, s : s + 1, :].astype(F32), (BLOCK, BLOCK))
                bias[i * BLOCK : (i + 1) * BLOCK, j * BLOCK : (j + 1) * BLOCK] = jnp.where(
                    column == row, 0.0, HIDDEN
                )
            bias[i * BLOCK : (i + 1) * BLOCK, TOKENS:] = jnp.broadcast_to(
                write_bias[0:1, TOKENS:], (BLOCK, BLOCK)
            )
        for copy in row_copies[s]:
            copy.wait_recv()
        if s < SEGS - 1:
            mixed = attend(kv[s, TOKENS : TOKENS + PAD, :], write_bias, s, TOKENS, PAD)
            owsend[s] = mixed
            ow[s, pl.ds(z, 1)] = mixed[None]
            write_copies = [
                push(started, owsend.at[s], ow.at[s, z], m_s.at[s, d - 1], m_r.at[s, d - 1], d)
                for d in (1, 2, 3)
            ]

        def block(i, carry):
            row_at = pl.multiple_of(i * BLOCK, BLOCK)
            rows = pl.ds(row_at, BLOCK)
            osend[s, i] = attend(kv[s, rows, :], bias[rows, :], s, row_at, BLOCK)
            return carry

        lax.fori_loop(0, 4, block, 0)
        part = slice(s * BLOCK, (s + 1) * BLOCK)
        out_copies += [
            push(
                started, osend.at[s, ring(d)], orow.at[z, part],
                o_s.at[s, d - 1], o_r.at[s, d - 1], d,
            )
            for d in (1, 2, 3)
        ]
        orow[z, part, :] = osend[s, z]
        if s < SEGS - 1:
            if s == 0:
                for copy in fetched[3:]:
                    copy.wait()
            for copy in write_copies:
                copy.wait_recv()
            hidden = xm[s, 0:PAD, :].astype(F32) + vec[MIXER_B : MIXER_B + 1, :]
            for g in range(4):
                hidden = hidden + dot(ow[s, g], wm[g * GROUP : (g + 1) * GROUP, :])
            h1w[s] = hidden
            unit, _ = norm_parts(hidden)
            upper = unit * vec[GAIN_1 : GAIN_1 + 1, :] + vec[SHIFT_1 : SHIFT_1 + 1, :]
            inner = dot(upper.astype(LOW), wi[...]) + inner_b[...]
            zw[s] = inner
            active, _ = gelu_parts(inner)
            hidden = upper + dot(active.astype(LOW), wo[...]) + vec[OUTER_B : OUTER_B + 1, :]
            h2w[s] = hidden
            unit, _ = norm_parts(hidden)
            result = unit * vec[GAIN_2 : GAIN_2 + 1, :] + vec[SHIFT_2 : SHIFT_2 + 1, :]
            flag = jnp.full((PAD, MODEL), resets[0, s], jnp.int32)
            result = jnp.where(flag > 0, init[...].astype(F32), result)
            memory = jnp.where(slot < SLOTS, result, 0.0).astype(LOW)
    for copy in out_copies:
        copy.wait_recv()
    for copy in started:
        copy.wait_send()


def shape(dims, kind=LOW):
    return jax.ShapeDtypeStruct(dims, kind)


VMEM = pl.BlockSpec(memory_space=pltpu.VMEM)
ANY = pl.BlockSpec(memory_space=pl.ANY)
DMA = pltpu.SemaphoreType.DMA


def weight_buffers():
    return [pltpu.VMEM((MODEL, MODEL), LOW) for _ in range(4)] + [
        pltpu.VMEM((MODEL, INNER), LOW),
        pltpu.VMEM((INNER, MODEL), LOW),
    ]


def forward(resets, tok, docs, init, offset, vec, inner_b, weights):
    return pl.pallas_call(
        forward_kernel,
        out_shape=(
            shape((SEGS, KEYS, TRIPLE)),
            shape((SEGS, MINE, QUERIES, KEYS)),
            shape((4, ROWS, GROUP)),
            shape((2, 4, PAD, GROUP)),
            shape((2, PAD, MODEL), F32),
            shape((2, PAD, INNER), F32),
            shape((2, PAD, MODEL), F32),
            shape((SEGS, MEMORY, MODEL)),
        ),
        in_specs=[pl.BlockSpec(memory_space=pltpu.SMEM)] + [VMEM] * 6 + [ANY] * 6,
        out_specs=(VMEM,) * 8,
        scratch_shapes=weight_buffers()
        + [
            pltpu.VMEM((MODEL, TRIPLE), LOW),
            pltpu.VMEM((8, TRIPLE), F32),
            pltpu.VMEM((4, SEGS, BLOCK, TRIPLE), LOW),
            pltpu.VMEM((4, SEGS, BLOCK), jnp.int32),
            pltpu.VMEM((TOKENS, KEYS), F32),
            pltpu.VMEM((SEGS, 4, BLOCK, GROUP), LOW),
            pltpu.VMEM((2, PAD, GROUP), LOW),
            DMA((6,)),
            DMA((SEGS, 3)),
            DMA((SEGS, 3)),
            DMA((SEGS, 3)),
            DMA((SEGS, 3)),
            DMA((2, 3)),
            DMA((2, 3)),
            DMA((3,)),
            DMA((3,)),
        ],
        compiler_params=pltpu.CompilerParams(
            collective_id=1, has_side_effects=True, vmem_limit_bytes=60 << 20
        ),
        name="forward_attention",
    )(resets, tok, docs, init, offset, vec, inner_b, *weights)


WIDE = 768
HALF = 4608
PART = 1536
CHUNK = 384
SUB = 96
ORDERS = (("x", "y", "z"), ("y", "z", "x"), ("z", "x", "y"))


def places():
    chain = lax.axis_index("chain")
    return {
        "x": chain // 8,
        "y": lax.rem(chain // 2, 4),
        "z": lax.axis_index("seq"),
        "core": lax.rem(chain, 2),
    }


def peer(at, axis, off):
    at = dict(at)
    size = 2 if axis == "core" else 4
    at[axis] = lax.rem(at[axis] + off + size, size)
    return ((at["x"] * 4 + at["y"]) * 2 + at["core"], at["z"])


def greet(at, peers):
    barrier = pltpu.get_barrier_semaphore()
    for axis, off in peers:
        pl.semaphore_signal(barrier, inc=1, device_id=peer(at, axis, off), device_id_type=MESH)
    pl.semaphore_wait(barrier, len(peers))


ALL_PEERS = [("core", 1)] + [(axis, off) for axis in "xyz" for off in (1, 2, 3)]


def add_rows(out, out_start, terms, rows, step=48):
    def body(i, carry):
        base = i * step
        total = None
        for ref, start in terms:
            term = ref[pl.ds(pl.multiple_of(start + base, 16), step), :].astype(jnp.float32)
            total = term if total is None else total + term
        out[pl.ds(pl.multiple_of(out_start + base, 16), step), :] = total.astype(out.dtype)
        return carry

    lax.fori_loop(0, rows // step, body, 0)


def sum_kernel(
    g, ext, w, e, crecv, r1, r2, r3, r4, ecore, ex, ey, ez,
    c_s, c_r, a1_s, a1_r, a2_s, a2_r, b_s, b_r, d_s, d_r,
    gd_s, gd_r, gb_s, gb_r, g1_s, g1_r, g2_s, g2_r, gc_s, gc_r,
    e_s, e_r,
):
    at = places()
    greet(at, ALL_PEERS)
    started = []

    def send(src, dst, s_sem, r_sem, axis, off):
        copy = pltpu.make_async_remote_copy(
            src_ref=src, dst_ref=dst, send_sem=s_sem, recv_sem=r_sem,
            device_id=peer(at, axis, off), device_id_type=MESH,
        )
        copy.start()
        started.append(copy)
        return copy

    core = at["core"]
    mine = core * HALF
    theirs = (1 - core) * HALF

    def turn(value, off):
        return lax.rem(value + off + 4, 4)

    def ds(start, size):
        return pl.ds(pl.multiple_of(start, 16), size)

    place1 = [at[order[0]] for order in ORDERS]
    place2 = [at[order[1]] for order in ORDERS]
    place3 = [at[order[2]] for order in ORDERS]

    def rel(p, off):
        return p * PART + turn(place1[p], off) * CHUNK

    core_copies = {}
    e_core = send(
        ext.at[pl.ds(pl.multiple_of((1 - core) * 32, 8), 32)], ecore, e_s.at[0], e_r.at[0], "core", 1
    )
    for j, off in enumerate((2, 1, 3, 0)):
        for p in range(3):
            start = rel(p, off)
            core_copies[p, off] = send(
                g.at[ds(theirs + start, CHUNK)], crecv.at[ds(start, CHUNK)],
                c_s.at[p, j], c_r.at[p, j], "core", 1,
            )

    def own(p, off):
        core_copies[p, off].wait_recv()
        start = rel(p, off)
        add_rows(crecv, start, [(g, mine + start), (crecv, start)], CHUNK)

    e_core.wait_recv()
    ecore[...] = ext[pl.ds(pl.multiple_of(core * 32, 8), 32), :] + ecore[...]
    e_x = [
        send(
            ecore.at[pl.ds(pl.multiple_of(turn(at["x"], d) * 8, 8), 8)],
            ex.at[d - 1], e_s.at[d], e_r.at[d], "x", d,
        )
        for d in (1, 2, 3)
    ]
    first = {}
    for p in range(3):
        own(p, 2)
        start = rel(p, 2)
        axis = ORDERS[p][0]
        first[p] = (
            send(crecv.at[ds(start, CHUNK // 2)], r1.at[p, 0], a1_s.at[p, 0], a1_r.at[p, 0], axis, 1),
            send(
                crecv.at[ds(start + CHUNK // 2, CHUNK // 2)], r1.at[p, 1],
                a1_s.at[p, 1], a1_r.at[p, 1], axis, 3,
            ),
        )
    for off in (1, 3, 0):
        for p in range(3):
            own(p, off)
    second = {}
    for p in range(3):
        axis = ORDERS[p][0]
        start = rel(p, 1)
        first[p][0].wait_recv()
        add_rows(crecv, start, [(crecv, start), (r1.at[p, 0], 0)], CHUNK // 2)
        right = send(crecv.at[ds(start, CHUNK)], r2.at[p, 0], a2_s.at[p, 0], a2_r.at[p, 0], axis, 1)
        start = rel(p, 3)
        first[p][1].wait_recv()
        add_rows(
            crecv, start + CHUNK // 2, [(crecv, start + CHUNK // 2), (r1.at[p, 1], 0)], CHUNK // 2
        )
        left = send(crecv.at[ds(start, CHUNK)], r2.at[p, 1], a2_s.at[p, 1], a2_r.at[p, 1], axis, 3)
        second[p] = (right, left)
    e_own = pl.ds(pl.multiple_of(core * 32 + at["x"] * 8, 8), 8)
    for copy in e_x:
        copy.wait_recv()
    ey[pl.ds(at["y"], 1)] = (ecore[pl.ds(pl.multiple_of(at["x"] * 8, 8), 8), :] + ex[0] + ex[1] + ex[2])[None]
    e_y = [
        send(ey.at[at["y"]], ey.at[at["y"]], e_s.at[3 + d], e_r.at[3 + d], "y", d)
        for d in (1, 2, 3)
    ]
    third = {}
    for p in range(3):
        start = rel(p, 0)
        for copy in second[p]:
            copy.wait_recv()
        add_rows(crecv, start, [(crecv, start), (r2.at[p, 0], 0), (r2.at[p, 1], 0)], CHUNK)
        third[p] = [
            send(
                crecv.at[ds(start + turn(place2[p], d) * SUB, SUB)], r3.at[p, d - 1],
                b_s.at[p, d - 1], b_r.at[p, d - 1], ORDERS[p][1], d,
            )
            for d in (1, 2, 3)
        ]
    for copy in e_y:
        copy.wait_recv()
    ez[pl.ds(at["z"], 1)] = (ey[0] + ey[1] + ey[2] + ey[3])[None]
    e_z = [
        send(ez.at[at["z"]], ez.at[at["z"]], e_s.at[6 + d], e_r.at[6 + d], "z", d)
        for d in (1, 2, 3)
    ]
    fourth = {}

    def quarter(ref, start, c):
        return ref.at[ds(start + (c // 2) * (SUB // 2), SUB // 2), pl.ds(pl.multiple_of(lax.rem(c, 2) * (WIDE // 2), 128), WIDE // 2)]

    for p in range(3):
        start = rel(p, 0) + place2[p] * SUB
        for copy in third[p]:
            copy.wait_recv()
        add_rows(crecv, start, [(crecv, start)] + [(r3.at[p, d], 0) for d in range(3)], SUB)
        fourth[p] = [
            send(
                quarter(crecv, start, turn(place3[p], d)), r4.at[p, d - 1],
                d_s.at[p, d - 1], d_r.at[p, d - 1], ORDERS[p][2], d,
            )
            for d in (1, 2, 3)
        ]
    for copy in e_z:
        copy.wait_recv()
    e[e_own, :] = ez[0] + ez[1] + ez[2] + ez[3]
    e_back = [
        send(e.at[e_own], e.at[e_own], e_s.at[9 + d], e_r.at[9 + d], "x", d) for d in (1, 2, 3)
    ]
    fifth = {}
    for p in range(3):
        start = rel(p, 0) + place2[p] * SUB
        for copy in fourth[p]:
            copy.wait_recv()
        total = quarter(crecv, start, place3[p])[...].astype(jnp.float32)
        for d in range(3):
            total = total + r4[p, d].astype(jnp.float32)
        piece = quarter(w, mine + start, place3[p])
        piece[...] = total.astype(w.dtype)
        fifth[p] = [
            send(piece, piece, gd_s.at[p, d - 1], gd_r.at[p, d - 1], ORDERS[p][2], d)
            for d in (1, 2, 3)
        ]
    sixth = {}
    for p in range(3):
        start = mine + rel(p, 0) + place2[p] * SUB
        for copy in fifth[p]:
            copy.wait_recv()
        piece = w.at[ds(start, SUB)]
        sixth[p] = [
            send(piece, piece, gb_s.at[p, d - 1], gb_r.at[p, d - 1], ORDERS[p][1], d)
            for d in (1, 2, 3)
        ]
    for copy in e_back:
        copy.wait_recv()
    e_half = e.at[pl.ds(pl.multiple_of(core * 32, 8), 32)]
    e_last = send(e_half, e_half, e_s.at[13], e_r.at[13], "core", 1)
    seventh = {}
    last = []

    def across(p, j, start, rows):
        piece = w.at[ds(start, rows)]
        last.append(send(piece, piece, gc_s.at[p, j], gc_r.at[p, j], "core", 1))

    for p in range(3):
        start = mine + rel(p, 0)
        for copy in sixth[p]:
            copy.wait_recv()
        piece = w.at[ds(start, CHUNK)]
        axis = ORDERS[p][0]
        seventh[p] = (
            send(piece, piece, g1_s.at[p, 0], g1_r.at[p, 0], axis, 1),
            send(piece, piece, g1_s.at[p, 1], g1_r.at[p, 1], axis, 3),
        )
        across(p, 0, start, CHUNK)
    eighth = {}
    for p in range(3):
        axis = ORDERS[p][0]
        seventh[p][0].wait_recv()
        start = mine + rel(p, 3)
        piece = w.at[ds(start, CHUNK // 2)]
        right = send(piece, piece, g2_s.at[p, 0], g2_r.at[p, 0], axis, 1)
        across(p, 1, start, CHUNK)
        seventh[p][1].wait_recv()
        start = mine + rel(p, 1)
        piece = w.at[ds(start + CHUNK // 2, CHUNK // 2)]
        left = send(piece, piece, g2_s.at[p, 1], g2_r.at[p, 1], axis, 3)
        across(p, 2, start, CHUNK)
        eighth[p] = (right, left)
    for p in range(3):
        start = mine + rel(p, 2)
        for i in range(2):
            eighth[p][i].wait_recv()
            across(p, 3 + i, start + i * (CHUNK // 2), CHUNK // 2)
    e_last.wait_recv()
    for copy in last:
        copy.wait_recv()
    for copy in started:
        copy.wait_send()


def sum_all(g, ext):
    dma = pltpu.SemaphoreType.DMA
    pairs = [(3, 4), (3, 2), (3, 2), (3, 3), (3, 3), (3, 3), (3, 3), (3, 2), (3, 2), (3, 5), (14,)]
    sems = [dma(shape) for shape in pairs for _ in range(2)]
    vmem = pl.BlockSpec(memory_space=pltpu.VMEM)
    return pl.pallas_call(
        sum_kernel,
        out_shape=(
            jax.ShapeDtypeStruct((2 * HALF, WIDE), jnp.bfloat16),
            jax.ShapeDtypeStruct((64, WIDE), jnp.float32),
        ),
        in_specs=[vmem, vmem],
        out_specs=(vmem, vmem),
        scratch_shapes=[
            pltpu.VMEM((HALF, WIDE), jnp.bfloat16),
            pltpu.VMEM((3, 2, CHUNK // 2, WIDE), jnp.bfloat16),
            pltpu.VMEM((3, 2, CHUNK, WIDE), jnp.bfloat16),
            pltpu.VMEM((3, 3, SUB, WIDE), jnp.bfloat16),
            pltpu.VMEM((3, 3, SUB // 2, WIDE // 2), jnp.bfloat16),
            pltpu.VMEM((32, WIDE), jnp.float32),
            pltpu.VMEM((3, 8, WIDE), jnp.float32),
            pltpu.VMEM((4, 8, WIDE), jnp.float32),
            pltpu.VMEM((4, 8, WIDE), jnp.float32),
        ] + sems,
        compiler_params=pltpu.CompilerParams(
            collective_id=7, has_side_effects=True, vmem_limit_bytes=60 << 20
        ),
        name="sum_all",
    )(g, ext)


def middle_kernel(
    tok, orow, cot, vec, inner_b, wm_h, wi_h, wo_h,
    out, ub, act, dz, df, da, dh1, dout, sums, inner_sum,
    wm, wi, wo, slope, total, unit_1, inverse_1, w_sem,
):
    fetched = fetch([(wm_h, wm), (wi_h, wi), (wo_h, wo)], w_sem)
    gain_1 = vec[GAIN_1 : GAIN_1 + 1, :]
    gain_2 = vec[GAIN_2 : GAIN_2 + 1, :]
    hidden = tok[...].reshape(ROWS, MODEL).astype(F32) + vec[MIXER_B : MIXER_B + 1, :]
    fetched[0].wait()
    for g in range(4):
        hidden = hidden + dot(orow[g], wm[g * GROUP : (g + 1) * GROUP, :])
    unit, inverse = norm_parts(hidden)
    unit_1[...] = unit
    inverse_1[...] = inverse
    upper = unit * gain_1 + vec[SHIFT_1 : SHIFT_1 + 1, :]
    ub[...] = upper.astype(LOW)
    total[...] = upper + vec[OUTER_B : OUTER_B + 1, :]
    for copy in fetched[1:]:
        copy.wait()

    def ahead(j, carry):
        cut = pl.ds(pl.multiple_of(j * MODEL, MODEL), MODEL)
        inner = dot(ub[...], wi[:, cut]) + inner_b[:, cut]
        active, slant = gelu_parts(inner)
        active = active.astype(LOW)
        act[:, cut] = active
        slope[:, cut] = slant
        total[...] += dot(active, wo[cut, :])
        return carry

    lax.fori_loop(0, INNER // MODEL, ahead, 0)
    unit, inverse = norm_parts(total[...])
    result = unit * gain_2 + vec[SHIFT_2 : SHIFT_2 + 1, :]
    out[...] = result.astype(LOW).reshape(1, SEGS, BLOCK, MODEL)
    upstream = cot[...].reshape(ROWS, MODEL).astype(F32)
    sums[GAIN_2 : GAIN_2 + 1, :] = column_sum(upstream * unit)
    sums[SHIFT_2 : SHIFT_2 + 1, :] = column_sum(upstream)
    d_hidden = norm_back(upstream, unit, inverse, gain_2)
    total[...] = d_hidden
    d_low = d_hidden.astype(LOW)
    df[...] = d_low
    sums[OUTER_B : OUTER_B + 1, :] = column_sum(d_low)

    def back(j, carry):
        cut = pl.ds(pl.multiple_of(j * MODEL, MODEL), MODEL)
        d_inner = (dot_t(df[...], wo[cut, :]) * slope[:, cut]).astype(LOW)
        dz[:, cut] = d_inner
        inner_sum[:, cut] = column_sum(d_inner)
        total[...] += dot_t(d_inner, wi[:, cut])
        return carry

    lax.fori_loop(0, INNER // MODEL, back, 0)
    upstream = total[...]
    unit = unit_1[...]
    sums[GAIN_1 : GAIN_1 + 1, :] = column_sum(upstream * unit)
    sums[SHIFT_1 : SHIFT_1 + 1, :] = column_sum(upstream)
    d_hidden = norm_back(upstream, unit, inverse_1[...], gain_1)
    dh1[...] = d_hidden
    d_low = d_hidden.astype(LOW)
    da[...] = d_low
    sums[MIXER_B : MIXER_B + 1, :] = column_sum(d_low)
    sums[QUERY_B : QUERY_B + 2, :] = jnp.zeros((2, MODEL), F32)
    for g in range(4):
        dout[g] = dot_t(d_low, wm[g * GROUP : (g + 1) * GROUP, :]).astype(LOW)


def middle(tok, orow, cot, vec, inner_b, weights):
    return pl.pallas_call(
        middle_kernel,
        out_shape=(
            shape((1, SEGS, BLOCK, MODEL)),
            shape((ROWS, MODEL)),
            shape((ROWS, INNER)),
            shape((ROWS, INNER)),
            shape((ROWS, MODEL)),
            shape((ROWS, MODEL)),
            shape((ROWS, MODEL), F32),
            shape((4, ROWS, GROUP)),
            shape((8, MODEL), F32),
            shape((1, INNER), F32),
        ),
        in_specs=[VMEM] * 5 + [ANY] * 3,
        out_specs=(VMEM,) * 10,
        scratch_shapes=[
            pltpu.VMEM((MODEL, MODEL), LOW),
            pltpu.VMEM((MODEL, INNER), LOW),
            pltpu.VMEM((INNER, MODEL), LOW),
            pltpu.VMEM((ROWS, INNER), F32),
            pltpu.VMEM((ROWS, MODEL), F32),
            pltpu.VMEM((ROWS, MODEL), F32),
            pltpu.VMEM((ROWS, 1), F32),
            DMA((3,)),
        ],
        compiler_params=pltpu.CompilerParams(vmem_limit_bytes=60 << 20),
        name="token_layer",
    )(tok, orow, cot, vec, inner_b, *weights[3:])


def backward_kernel(
    resets, dout, kv, probs, h1w, zw, h2w, vec,
    wq_h, wk_h, wv_h, wm_h, wi_h, wo_h,
    drow, dmem, ubw, gw, dzw, dfw, daw, small,
    wq, wk, wv, wm, wi, wo, doh, dow, ds, acc, dsend, msend, wide,
    w_sem, d_s, d_r, x_s, x_r, m_s, m_r,
):
    z = lax.axis_index("seq")
    fetched = fetch(
        [(wq_h, wq), (wk_h, wk), (wv_h, wv), (wm_h, wm), (wi_h, wi), (wo_h, wo)], w_sem
    )
    started = []
    ring_barrier()
    here = pl.ds(pl.multiple_of(z * BLOCK, BLOCK), BLOCK)
    in_copies = {}
    for s in reversed(range(SEGS)):
        part = slice(s * BLOCK, (s + 1) * BLOCK)
        in_copies[s] = [
            push(
                started, dout.at[ring(d), part], doh.at[s, here],
                d_s.at[s, d - 1], d_r.at[s, d - 1], d,
            )
            for d in (1, 2, 3)
        ]
        doh[s, here, :] = dout[z, part, :]
    gain_1 = vec[GAIN_1 : GAIN_1 + 1, :]
    gain_2 = vec[GAIN_2 : GAIN_2 + 1, :]

    def head_back(s, h, d_rows, rows):
        cut = slice(h * HEAD, (h + 1) * HEAD)
        key_head = kv[s, :, GROUP + h * HEAD : GROUP + (h + 1) * HEAD]
        value_head = kv[s, :, 2 * GROUP + h * HEAD : 2 * GROUP + (h + 1) * HEAD]
        d_head = d_rows[:, cut]
        prob = probs[s, h, rows, :]
        wide_prob = prob.astype(F32)
        product = wide_prob * dot_t(d_head, value_head)
        delta = jnp.sum(product, axis=-1, keepdims=True)
        d_scores = (product - wide_prob * delta).astype(LOW)
        d_query = (dot(d_scores, key_head) * SCALE).astype(LOW)
        d_key = t_dot(d_scores, kv[s, rows, cut])
        d_value = t_dot(prob, d_head)
        return d_query, d_key, d_value

    def tokens_back(s):
        for copy in in_copies[s]:
            copy.wait_recv()
        rows = slice(0, TOKENS)
        for h in range(MINE):
            cut = slice(h * HEAD, (h + 1) * HEAD)
            d_query, d_key, d_value = head_back(s, h, doh[s], rows)
            dsend[s, :, cut] = d_query
            acc[s, :, cut] = d_key
            acc[s, :, GROUP + h * HEAD : GROUP + (h + 1) * HEAD] = d_value

    def writes_back(s):
        rows = slice(TOKENS, TOKENS + PAD)
        for h in range(MINE):
            cut = slice(h * HEAD, (h + 1) * HEAD)
            d_query, d_key, d_value = head_back(s, h, dow[...], rows)
            msend[s, 0:PAD, cut] = d_query
            acc[s, :, cut] += d_key
            acc[s, :, GROUP + h * HEAD : GROUP + (h + 1) * HEAD] += d_value

    mem_copies = {}
    row_copies = []

    def finish(s):
        if s == SEGS - 1:
            msend[s, :, 0:GROUP] = jnp.zeros((MEMORY, GROUP), LOW)
        else:
            msend[s, PAD:, 0:GROUP] = jnp.zeros((PAD, GROUP), LOW)
        msend[s, :, GROUP:] = acc[s, TOKENS : TOKENS + MEMORY, :].astype(LOW)
        mem_copies[s] = [
            push(started, msend.at[s], dmem.at[s, z], m_s.at[s, d - 1], m_r.at[s, d - 1], d)
            for d in (1, 2, 3)
        ]
        dmem[s, z] = msend[s]
        dsend[s, :, GROUP:] = acc[s, 0:TOKENS, :].astype(LOW)
        part = slice(s * BLOCK, (s + 1) * BLOCK)
        for d in (1, 2, 3):
            there = pl.ds(pl.multiple_of(ring(d) * BLOCK, BLOCK), BLOCK)
            row_copies.append(
                push(
                    started, dsend.at[s, there], drow.at[z, part],
                    x_s.at[s, d - 1], x_r.at[s, d - 1], d,
                )
            )
        drow[z, part, :] = dsend[s, here, :]

    sums = {}

    def add(name, value):
        sums[name] = value if name not in sums else sums[name] + value

    saved = {}

    def memory_back(s):
        for copy in mem_copies[s]:
            copy.wait_recv()
        for g in range(4):
            for t in range(3):
                wide[t, :, g * GROUP : (g + 1) * GROUP] = dmem[
                    s, g, :, t * GROUP : (t + 1) * GROUP
                ]
        if s == SEGS - 1:
            for copy in fetched:
                copy.wait()
        d_rows = dot_t(wide[0], wq[...]) + dot_t(wide[1], wk[...]) + dot_t(wide[2], wv[...])
        write = d_rows[0:PAD]
        if s < SEGS - 1:
            write = write + saved[s]
        grad = write + d_rows[PAD:]
        add("offset", write)
        add("norm", jnp.sum(jnp.sum(grad * grad, axis=0, keepdims=True), axis=1, keepdims=True))
        if s == 0:
            add("init", grad)
            return None
        flag = jnp.full((PAD, MODEL), resets[0, s - 1], jnp.int32) > 0
        add("init", jnp.where(flag, grad, 0.0))
        return jnp.where(flag, 0.0, grad)

    def layer_back(s, upstream):
        unit, inverse = norm_parts(h2w[s])
        add("gain_2", column_sum(upstream * unit))
        add("shift_2", column_sum(upstream))
        d_second = norm_back(upstream, unit, inverse, gain_2)
        d_low = d_second.astype(LOW)
        dfw[s] = d_low
        add("outer", column_sum(d_low))
        active, slant = gelu_parts(zw[s])
        gw[s] = active.astype(LOW)
        d_inner = (dot_t(d_low, wo[...]) * slant).astype(LOW)
        dzw[s] = d_inner
        add("inner", column_sum(d_inner))
        unit, inverse = norm_parts(h1w[s])
        ubw[s] = (unit * gain_1 + vec[SHIFT_1 : SHIFT_1 + 1, :]).astype(LOW)
        d_upper = dot_t(d_inner, wi[...]) + d_second
        add("gain_1", column_sum(d_upper * unit))
        add("shift_1", column_sum(d_upper))
        d_first = norm_back(d_upper, unit, inverse, gain_1)
        saved[s] = d_first
        d_low = d_first.astype(LOW)
        daw[s] = d_low
        add("mixer", column_sum(d_low))
        own = pl.ds(pl.multiple_of(z * GROUP, HEAD), GROUP)
        dow[...] = dot_t(d_low, wm[own, :]).astype(LOW)

    tokens_back(2)
    finish(2)
    tokens_back(1)
    layer_back(1, memory_back(2))
    writes_back(1)
    finish(1)
    tokens_back(0)
    layer_back(0, memory_back(1))
    writes_back(0)
    finish(0)
    memory_back(0)
    quarter = 0.25
    row = lax.broadcasted_iota(jnp.int32, (24, MODEL), 0)
    zero = jnp.zeros((1, MODEL), F32)
    small[0:8, :] = quarter * jnp.concatenate(
        [zero, zero]
        + [sums[n] for n in ("mixer", "gain_1", "shift_1", "outer", "gain_2", "shift_2")],
        axis=0,
    )
    small[8:16, :] = quarter * jnp.concatenate(
        [sums["inner"][:, i * MODEL : (i + 1) * MODEL] for i in range(4)] + [zero] * 4, axis=0
    )
    small[16:40, :] = quarter * sums["init"][0:24]
    small[40:64, :] = quarter * (
        sums["offset"][0:24]
        + jnp.where(row >= SLOTS, jnp.broadcast_to(sums["norm"], (24, MODEL)), 0.0)
    )
    for copy in row_copies:
        copy.wait_recv()
    for copy in started:
        copy.wait_send()


def backward(resets, dout, kv, probs, h1w, zw, h2w, vec, weights):
    return pl.pallas_call(
        backward_kernel,
        out_shape=(
            shape((4, ROWS, TRIPLE)),
            shape((SEGS, 4, MEMORY, TRIPLE)),
            shape((2, PAD, MODEL)),
            shape((2, PAD, INNER)),
            shape((2, PAD, INNER)),
            shape((2, PAD, MODEL)),
            shape((2, PAD, MODEL)),
            shape((64, MODEL), F32),
        ),
        in_specs=[pl.BlockSpec(memory_space=pltpu.SMEM)] + [VMEM] * 7 + [ANY] * 6,
        out_specs=(VMEM,) * 8,
        scratch_shapes=weight_buffers()
        + [
            pltpu.VMEM((SEGS, TOKENS, GROUP), LOW),
            pltpu.VMEM((PAD, GROUP), LOW),
            pltpu.VMEM((TOKENS, KEYS), LOW),
            pltpu.VMEM((SEGS, KEYS, 2 * GROUP), F32),
            pltpu.VMEM((SEGS, TOKENS, TRIPLE), LOW),
            pltpu.VMEM((SEGS, MEMORY, TRIPLE), LOW),
            pltpu.VMEM((3, MEMORY, MODEL), LOW),
            DMA((6,)),
            DMA((SEGS, 3)),
            DMA((SEGS, 3)),
            DMA((SEGS, 3)),
            DMA((SEGS, 3)),
            DMA((SEGS, 3)),
            DMA((SEGS, 3)),
        ],
        compiler_params=pltpu.CompilerParams(
            collective_id=2, has_side_effects=True, vmem_limit_bytes=60 << 20
        ),
        name="backward_attention",
    )(resets, dout, kv, probs, h1w, zw, h2w, vec, *weights)


FULL = ROWS + MEMORY
MOST = ROWS + PAD


def weight_kernel(
    tok, xm, drow, dmem, orow, ow, dh1, sums, inner_sum, small, ubw, gw, dzw, dfw, daw,
    ub_h, act_h, dz_h, df_h, da_h, wq_h, wk_h, wv_h,
    packed, input_grad, ext,
    ub, act, dz, df, da, wq, wk, wv, rows, triple, mixed, w_sem,
):
    z = lax.axis_index("seq")
    top = pl.ds(0, ROWS)
    fetched = fetch(
        [
            (wq_h, wq), (wk_h, wk), (wv_h, wv), (da_h, da.at[top]), (ub_h, ub.at[top]),
            (dz_h, dz.at[top]), (df_h, df.at[top]), (act_h, act.at[top]),
        ],
        w_sem,
    )
    at = jnp.minimum(z, 2)
    keep = (z < SEGS).astype(F32).astype(LOW)
    low_at = jnp.minimum(z, 1)
    low_keep = (z < 2).astype(F32).astype(LOW)
    rows[0:ROWS, :] = tok[...].reshape(ROWS, MODEL)
    rows[ROWS:, :] = xm[at]
    for g in range(4):
        for t in range(3):
            cut = slice(g * GROUP, (g + 1) * GROUP)
            part = slice(t * GROUP, (t + 1) * GROUP)
            triple[t, 0:ROWS, cut] = drow[g, :, part]
            triple[t, ROWS:, cut] = dmem[at, g, :, part] * keep
        mixed[g, 0:ROWS, :] = orow[g]
        mixed[g, ROWS:, :] = ow[low_at, g]
    ub[ROWS:, :] = ubw[low_at]
    act[ROWS:, :] = gw[low_at]
    dz[ROWS:, :] = dzw[low_at] * low_keep
    df[ROWS:, :] = dfw[low_at] * low_keep
    da[ROWS:, :] = daw[low_at] * low_keep
    ext[...] = small[...]
    ext[0:8, :] += sums[...]
    ext[8:12, :] += jnp.concatenate(
        [inner_sum[:, i * MODEL : (i + 1) * MODEL] for i in range(4)], axis=0
    )
    ext[QUERY_B : QUERY_B + 1, :] += column_sum(triple[0])
    ext[VALUE_B : VALUE_B + 1, :] += column_sum(triple[2])
    for t in range(3):
        packed[t * MODEL : (t + 1) * MODEL, :] = t_dot(rows[...], triple[t]).astype(LOW)
    for copy in fetched[:4]:
        copy.wait()
    for g in range(4):
        start = 3 * MODEL + g * GROUP
        packed[start : start + GROUP, :] = t_dot(mixed[g], da[...]).astype(LOW)
    input_grad[...] = (
        dh1[...]
        + dot_t(triple[0, 0:ROWS, :], wq[...])
        + dot_t(triple[1, 0:ROWS, :], wk[...])
        + dot_t(triple[2, 0:ROWS, :], wv[...])
    ).reshape(1, SEGS, BLOCK, MODEL)
    for copy in fetched[4:]:
        copy.wait()

    def inner(j, carry):
        cut = pl.ds(pl.multiple_of(j * MODEL, MODEL), MODEL)
        there = pl.ds(pl.multiple_of((4 + j) * MODEL, MODEL), MODEL)
        packed[there, :] = t_dot(ub[...], dz[:, cut]).astype(LOW)
        there = pl.ds(pl.multiple_of((8 + j) * MODEL, MODEL), MODEL)
        packed[there, :] = t_dot(act[:, cut], df[...]).astype(LOW)
        return carry

    lax.fori_loop(0, 4, inner, 0)


def weight_sums(
    tok, xm, drow, dmem, orow, ow, dh1, sums, inner_sum, small, ubw, gw, dzw, dfw, daw,
    ub, act, dz, df, da, weights,
):
    return pl.pallas_call(
        weight_kernel,
        out_shape=(
            shape((12 * MODEL, MODEL)),
            shape((1, SEGS, BLOCK, MODEL), F32),
            shape((64, MODEL), F32),
        ),
        in_specs=[VMEM] * 15 + [ANY] * 8,
        out_specs=(VMEM,) * 3,
        scratch_shapes=[
            pltpu.VMEM((MOST, MODEL), LOW),
            pltpu.VMEM((MOST, INNER), LOW),
            pltpu.VMEM((MOST, INNER), LOW),
            pltpu.VMEM((MOST, MODEL), LOW),
            pltpu.VMEM((MOST, MODEL), LOW),
            pltpu.VMEM((MODEL, MODEL), LOW),
            pltpu.VMEM((MODEL, MODEL), LOW),
            pltpu.VMEM((MODEL, MODEL), LOW),
            pltpu.VMEM((FULL, MODEL), LOW),
            pltpu.VMEM((3, FULL, MODEL), LOW),
            pltpu.VMEM((4, MOST, GROUP), LOW),
            DMA((8,)),
        ],
        compiler_params=pltpu.CompilerParams(vmem_limit_bytes=60 << 20),
        name="weight_sums",
    )(
        tok, xm, drow, dmem, orow, ow, dh1, sums, inner_sum, small, ubw, gw, dzw, dfw, daw,
        ub, act, dz, df, da, *weights[:3],
    )


def shards(
    tokens, documents, resets, cotangent, query_weight, query_bias, key_weight, value_weight,
    value_bias, mixer_weight, mixer_bias, first_gain, first_shift, inner_weight, inner_bias,
    outer_weight, outer_bias, second_gain, second_shift, memory_init, write_offset,
):
    weights = (query_weight, key_weight, value_weight, mixer_weight, inner_weight, outer_weight)
    vec = jnp.stack(
        [
            query_bias, value_bias, mixer_bias, first_gain, first_shift, outer_bias, second_gain,
            second_shift,
        ]
    ).astype(F32)
    inner_b = inner_bias.astype(F32)[None]
    tok = tokens[0]
    spare = ((0, PAD - SLOTS), (0, 0))
    init = jnp.pad(memory_init, spare)
    offset = jnp.pad(write_offset, spare)
    kv, probs, orow, ow, h1w, zw, h2w, xm = forward(
        resets, tok, documents[0], init, offset, vec, inner_b, weights
    )
    layer_output, ub, act, dz, df, da, dh1, dout, sums, inner_sum = middle(
        tok, orow, cotangent[0], vec, inner_b, weights
    )
    drow, dmem, ubw, gw, dzw, dfw, daw, small = backward(
        resets, dout, kv, probs, h1w, zw, h2w, vec, weights
    )
    packed, input_grad, ext = weight_sums(
        tok, xm, drow, dmem, orow, ow, dh1, sums, inner_sum, small, ubw, gw, dzw, dfw, daw,
        ub, act, dz, df, da, weights,
    )
    packed, ext = sum_all(packed, ext)
    query_w, key_w, value_w, mixer_w = (
        packed[i * MODEL : (i + 1) * MODEL].astype(F32) for i in range(4)
    )
    inner_w = jnp.concatenate(
        [packed[i * MODEL : (i + 1) * MODEL] for i in range(4, 8)], axis=1
    ).astype(F32)
    outer_w = packed[8 * MODEL :].astype(F32)
    chains = lax.axis_size("chain")
    memory_norm = jnp.sqrt(ext[60, 0] / (chains * SEGS * SLOTS * MODEL))
    return (
        layer_output,
        input_grad,
        query_w,
        ext[QUERY_B],
        key_w,
        value_w,
        ext[VALUE_B],
        mixer_w,
        ext[MIXER_B],
        ext[GAIN_1],
        ext[SHIFT_1],
        inner_w,
        ext[8:12].reshape(-1),
        outer_w,
        ext[OUTER_B],
        ext[GAIN_2],
        ext[SHIFT_2],
        ext[16:36],
        ext[40:60],
        memory_norm,
    )


def solution(mesh):
    tokens = P("chain", None, "seq", None)
    in_specs = (tokens, P("chain", None, "seq"), P("chain", None), tokens) + (P(),) * 17
    out_specs = (tokens, tokens) + (P(),) * 18
    return jax.shard_map(shards, mesh=mesh, in_specs=in_specs, out_specs=out_specs, check_vma=False)
```

time: 819 us -> 290 us (0.35)
  waiting for transfers between devices: 288 us -> 0 us
  Pallas kernels: 0 us -> 248 us
  matrix products: 188 us -> 0 us
  blocking collectives: 155 us -> 0 us
  local copies, waits for them, and re-layouts: 93.6 us -> 17.2 us
  other arithmetic: 51.3 us -> 18 us
  between operations: 23.1 us -> 2.72 us
  starting transfers between devices: 15.1 us -> 0 us
    pallas_call x0 -> x5, Pallas kernels: none -> 248 us  [the longest x1 101 us: sum_all(): pl.pallas_call(sum_kernel, out_shape=(jax.ShapeDtypeStruct((2 * HALF, WID...]
    dot_general x72 -> x0, matrix products: 188 us -> none  [the longest x18 70 us: outer_sum(): lax.dot_general(left, right, (((0,), (0,)), ((), ())), preferred_element_...]
    psum x1 -> x0, waiting for transfers between devices: 150 us -> none  [shards(): lax.psum((totals['query_w'], totals['query_b'], totals['key_w'], totals['...]
    unnamed x7 -> x0, waiting for transfers between devices: 130 us -> none
    all_gather x7 -> x0, blocking collectives: 85.5 us -> none  [the longest x3 39.4 us: shards(): lax.all_gather(values, 'seq', axis=0, tiled=True)]
    psum x1 -> x0, blocking collectives: 69.1 us -> none  [shards(): lax.psum((totals['query_w'], totals['query_b'], totals['key_w'], totals['...]
    unnamed x536 -> x3, local copies, waits for them, and re-layouts: 36.9 us -> 3.1 us
    reduce_sum x30 -> x0, other arithmetic: 22.5 us -> none  [the longest x9 7.3 us: column_sum(): return jnp.sum(values.astype(jnp.float32), axis=0)]
  transfers between devices with their start and end apart: 9 -> 0, of which waited for: 8 -> 0; matrix products, arithmetic and copies ran while one was open for 11% -> 0% of each run, Pallas kernels for 0% -> 0%
where the time goes in v1:
time: 290 us; the launch traced here: 286 us
  Pallas kernels  248 us (86%)
  other arithmetic  18 us (6%)
  local copies, waits for them, and re-layouts  17.2 us (6%)
    pallas_call x1, Pallas kernels, sum_all(): pl.pallas_call(sum_kernel, out_shape=(jax.ShapeDtypeStruct((2 * HALF, WID...  101 us
    pallas_call x1, Pallas kernels, forward(): pl.pallas_call(forward_kernel, out_shape=(shape((SEGS, KEYS, TRIPLE)), sh...  59.4 us
    pallas_call x1, Pallas kernels, backward(): pl.pallas_call(backward_kernel, out_shape=(shape((4, ROWS, TRIPLE)), shap...  46.8 us
    pallas_call x1, Pallas kernels, middle(): pl.pallas_call(middle_kernel, out_shape=(shape((1, SEGS, BLOCK, MODEL)),...  20.6 us
    pallas_call x1, Pallas kernels, weight_sums(): pl.pallas_call(weight_kernel, out_shape=(shape((12 * MODEL, MODEL)), shap...  20.2 us
    convert_element_type x1, other arithmetic, shards(): outer_w = packed[8 * MODEL:].astype(F32)  8.01 us

profile of v1, /device:TPU:1, one launch (start us, length us, event | category | flops | bytes accessed | tf_op | source)
XLA Modules:
  0.0 285.7 jit_solution(13246884063345525437)
XLA Ops:
  0.7 1.3 copy.43
  1.9 0.7 stack.27
  2.6 0.7 stack.28
  3.3 0.7 stack.29
  4.0 0.7 stack.30
  4.7 0.7 stack.31
  5.3 0.7 stack.32
  6.0 0.7 stack.33
  6.7 0.7 stack.34
  7.4 0.6 convert_element_type.25.vec
  8.1 1.3 broadcast_in_dim.7
  9.4 1.4 pad.7.init
  10.7 1.4 pad.8.offset
  12.1 59.4 %forward_attention.1 = (bf16[3,640,576]{2,1,0:T(8,128)(2,1)}, bf16[3,3,544,640]{3,2,1,0:T(8,128)(2,1)}, bf16[4,384,192]{2,1,0:T(8,128)(2,1)}, bf16[2,4,32,192]{3...) custom-call(s32[1,2]{1,0:T(1,128)} %resets.3, ...), custom_call_target="tpu_custom_call" | custom-call | tf_op jit(solution)/shard_map/forward_attention/pallas_call | solution.py:287
  71.5 20.6 %token_layer.1 = (bf16[1,3,128,768]{3,2,1,0:T(8,128)(2,1)}, bf16[384,768]{1,0:T(8,128)(2,1)}, bf16[384,3072]{1,0:T(8,128)(2,1)}, bf16[384,3072]{1,0:T(8,128)(2,1...) custom-call(bf16[3,128,768]{2,1,0:T(8,128)(2,1)} %bitcast.8, ...), custom_call_target="tpu_custom_call" | custom-call | tf_op jit(solution)/shard_map/token_layer/pallas_call | solution.py:688
  92.1 46.8 %backward_attention.1 = (bf16[4,384,576]{2,1,0:T(8,128)(2,1)}, bf16[3,4,64,576]{3,2,1,0:T(8,128)(2,1)}, bf16[2,32,768]{2,1,0:T(8,128)(2,1)}, bf16[2,32,3072]{2,1...) custom-call(s32[1,2]{1,0:T(1,128)} %resets.3, ...), custom_call_target="tpu_custom_call" | custom-call | tf_op jit(solution)/shard_map/backward_attention/pallas_call | solution.py:900
  138.9 20.2 %weight_sums.1 = (bf16[9216,768]{1,0:T(8,128)(2,1)}, f32[1,3,128,768]{3,2,1,0:T(8,128)}, f32[64,768]{1,0:T(8,128)}) custom-call(bf16[3,128,768]{2,1,0:T(8,128)(2,1)} %bitcast.9, bf16[3,64,768]{2,1,0:T(8,128)(2,1)} %get-tuple-element.53.xm, bf16[4,384,576]{2,1,0:T(8,128)(2,1)} %get-tuple-element.60.drow, bf16[3,4,64,576]{3,2,1,0:T(8,128)(2,1)} %get-tuple-element.61.dmem, ...), custom_call_target="tpu_custom_call" | custom-call | tf_op jit(solution)/shard_map/weight_sums/pallas_call | solution.py:1014
  159.2 100.8 %sum_all.1 = (bf16[9216,768]{1,0:T(8,128)(2,1)}, f32[64,768]{1,0:T(8,128)}) custom-call(bf16[9216,768]{1,0:T(8,128)(2,1)} %get-tuple-element.78.g, f32[64,768]{1,0:T(8,128)} %get-tuple-element.79.ext), custom_call_target="tpu_custom_call" | custom-call | tf_op jit(solution)/shard_map/sum_all/pallas_call | solution.py:594
  259.9 1.2 slice.83
  261.8 0.7 slice.76
  262.6 0.6 reshape.46
  263.2 1.7 slice_reduce_fusion
  264.9 1.6 fusion.1
  266.5 0.0 copy-start
  266.5 8.0 %slice_convert_fusion = f32[3072,768]{1,0:T(8,128)} fusion(bf16[9216,768]{1,0:T(8,128)(2,1)} %get-tuple-element.80), kind=kLoop, calls=%fused_computation.1 | loop fusion | flops 2359296 | bytes 14155776 | tf_op jit(solution)/shard_map/convert_element_type | solution.py:1082
  274.5 1.8 copy-done
  276.3 3.8 %fusion = (bf16[768,768]{1,0:T(8,128)(2,1)S(1)}, bf16[768,768]{1,0:T(8,128)(2,1)S(1)}, bf16[768,768]{1,0:T(8,128)(2,1)S(1)}, bf16[768,768]{1,0:T(8,128)(2,1)S(1)...) fusion(bf16[9216,768]{1,0:T(8,128)(2,1)S(1)} %copy-done), kind=kLoop, calls=%fused_computation.15 | loop fusion | flops 2359296 | bytes 23592960 | tf_op jit(solution)/shard_map/slice | solution.py:1080
  280.1 4.3 %maximum_convert_fusion = f32[768,3072]{1,0:T(8,128)} fusion(bf16[768,768]{1,0:T(8,128)(2,1)S(1)} %get-tuple-element.91, bf16[768,768]{1,0:T(8,128)(2,1)S(1)} %get-tuple-element.92, bf16[768,768]{1,0:T(8,128)(2,1)S(1)} %get-tuple-element.93, bf16[768,768]{1,0:T(8,128)(2,1)S(1)} %get-tuple-element.90), kind=kLoop, calls=%fused_computation | loop fusion | flops 18874368 | bytes 14155776 | tf_op jit(solution)/shard_map/convert_element_type | solution.py:1081
  (1 shorter events, 0.0 us)
Async XLA Ops:
  266.5 9.8 %copy-start = (bf16[9216,768]{1,0:T(8,128)(2,1)S(1)}, bf16[9216,768]{1,0:T(8,128)(2,1)}, u32[]{:S(2)}) copy-start(bf16[9216,768]{1,0:T(8,128)(2,1)} %get-tuple-element.80) | copy-start | bytes 42467332

commit v2 on v1

--- a/solution.py
+++ b/solution.py
@@ -104,10 +104,10 @@
 
 
 def forward_kernel(
-    resets, tok, docs, init, offset, vec, inner_b,
-    wq_h, wk_h, wv_h, wm_h, wi_h, wo_h,
-    kv, probs, orow, ow, h1w, zw, h2w, xm,
-    wq, wk, wv, wm, wi, wo, wown, vown, sbuf, lab, bias, osend, owsend,
+    resets, tok, docs, init_in, offset_in, query_b, value_b, mixer_b, gain_1, shift_1, outer_b,
+    gain_2, shift_2, inner_in, wq_h, wk_h, wv_h, wm_h, wi_h, wo_h,
+    kv, probs, orow, ow, h1w, zw, h2w, xm, vec, inner_b,
+    wq, wk, wv, wm, wi, wo, wown, vown, sbuf, lab, bias, osend, owsend, init, offset,
     w_sem, q_s, q_r, o_s, o_r, m_s, m_r, l_s, l_r,
 ):
     z = lax.axis_index("seq")
@@ -115,6 +115,13 @@
         [(wq_h, wq), (wk_h, wk), (wv_h, wv), (wm_h, wm), (wi_h, wi), (wo_h, wo)], w_sem
     )
     started = []
+    vectors = (query_b, value_b, mixer_b, gain_1, shift_1, outer_b, gain_2, shift_2)
+    for i, ref in enumerate(vectors):
+        vec[i : i + 1, :] = ref[...].astype(F32).reshape(1, MODEL)
+    inner_b[...] = inner_in[...].astype(F32).reshape(1, INNER)
+    for wide, ref in ((init, init_in), (offset, offset_in)):
+        wide[...] = jnp.zeros((PAD, MODEL), LOW)
+        wide[0:SLOTS, :] = ref[...]
     ring_barrier()
     lab[pl.ds(z, 1)] = docs[...][None]
     label_copies = [
@@ -194,6 +201,17 @@
     memory = init[...]
     for copy in label_copies:
         copy.wait_recv()
+    for s in range(SEGS):
+        for i in range(4):
+            column = jnp.transpose(jnp.broadcast_to(lab[i, s : s + 1, :].astype(F32), (BLOCK, BLOCK)))
+            for j in range(4):
+                row = jnp.broadcast_to(lab[j, s : s + 1, :].astype(F32), (BLOCK, BLOCK))
+                bias[s, i * BLOCK : (i + 1) * BLOCK, j * BLOCK : (j + 1) * BLOCK] = jnp.where(
+                    column == row, 0.0, HIDDEN
+                )
+            bias[s, i * BLOCK : (i + 1) * BLOCK, TOKENS:] = jnp.broadcast_to(
+                write_bias[0:1, TOKENS:], (BLOCK, BLOCK)
+            )
     out_copies = []
     for s in range(SEGS):
         written_in = (memory.astype(F32) + offset[...].astype(F32)).astype(LOW)
@@ -202,16 +220,6 @@
         kv[s, TOKENS : TOKENS + MEMORY, :] = (
             (dot(xm[s], wown[...]) + vown[0:1, :]) * factor
         ).astype(LOW)
-        for i in range(4):
-            column = jnp.transpose(jnp.broadcast_to(lab[i, s : s + 1, :].astype(F32), (BLOCK, BLOCK)))
-            for j in range(4):
-                row = jnp.broadcast_to(lab[j, s : s + 1, :].astype(F32), (BLOCK, BLOCK))
-                bias[i * BLOCK : (i + 1) * BLOCK, j * BLOCK : (j + 1) * BLOCK] = jnp.where(
-                    column == row, 0.0, HIDDEN
-                )
-            bias[i * BLOCK : (i + 1) * BLOCK, TOKENS:] = jnp.broadcast_to(
-                write_bias[0:1, TOKENS:], (BLOCK, BLOCK)
-            )
         for copy in row_copies[s]:
             copy.wait_recv()
         if s < SEGS - 1:
@@ -226,7 +234,7 @@
         def block(i, carry):
             row_at = pl.multiple_of(i * BLOCK, BLOCK)
             rows = pl.ds(row_at, BLOCK)
-            osend[s, i] = attend(kv[s, rows, :], bias[rows, :], s, row_at, BLOCK)
+            osend[s, i] = attend(kv[s, rows, :], bias[s, rows, :], s, row_at, BLOCK)
             return carry
 
         lax.fori_loop(0, 4, block, 0)
@@ -283,7 +291,7 @@
     ]
 
 
-def forward(resets, tok, docs, init, offset, vec, inner_b, weights):
+def forward(resets, tok, docs, init, offset, vectors, inner_b, weights):
     return pl.pallas_call(
         forward_kernel,
         out_shape=(
@@ -295,18 +303,22 @@
             shape((2, PAD, INNER), F32),
             shape((2, PAD, MODEL), F32),
             shape((SEGS, MEMORY, MODEL)),
+            shape((8, MODEL), F32),
+            shape((1, INNER), F32),
         ),
-        in_specs=[pl.BlockSpec(memory_space=pltpu.SMEM)] + [VMEM] * 6 + [ANY] * 6,
-        out_specs=(VMEM,) * 8,
+        in_specs=[pl.BlockSpec(memory_space=pltpu.SMEM)] + [VMEM] * 13 + [ANY] * 6,
+        out_specs=(VMEM,) * 10,
         scratch_shapes=weight_buffers()
         + [
             pltpu.VMEM((MODEL, TRIPLE), LOW),
             pltpu.VMEM((8, TRIPLE), F32),
             pltpu.VMEM((4, SEGS, BLOCK, TRIPLE), LOW),
             pltpu.VMEM((4, SEGS, BLOCK), jnp.int32),
-            pltpu.VMEM((TOKENS, KEYS), F32),
+            pltpu.VMEM((SEGS, TOKENS, KEYS), F32),
             pltpu.VMEM((SEGS, 4, BLOCK, GROUP), LOW),
             pltpu.VMEM((2, PAD, GROUP), LOW),
+            pltpu.VMEM((PAD, MODEL), LOW),
+            pltpu.VMEM((PAD, MODEL), LOW),
             DMA((6,)),
             DMA((SEGS, 3)),
             DMA((SEGS, 3)),
@@ -321,7 +333,7 @@
             collective_id=1, has_side_effects=True, vmem_limit_bytes=60 << 20
         ),
         name="forward_attention",
-    )(resets, tok, docs, init, offset, vec, inner_b, *weights)
+    )(resets, tok, docs, init, offset, *vectors, inner_b, *weights)
 
 
 WIDE = 768
@@ -1042,25 +1054,84 @@
     )
 
 
+def widen_kernel(
+    count, packed, ext,
+    query_w, key_w, value_w, mixer_w, inner_w, outer_w, query_b, value_b, mixer_b, gain_1, shift_1,
+    inner_b, outer_b, gain_2, shift_2, init, offset, norm,
+    low, wide, in_sem, out_sem,
+):
+    def rows(i):
+        return pl.ds(i * MODEL, MODEL)
+
+    loads = [pltpu.make_async_copy(packed.at[rows(i)], low.at[i], in_sem.at[i]) for i in range(12)]
+    for copy in loads:
+        copy.start()
+    targets = [query_w, key_w, value_w, mixer_w]
+    targets += [inner_w.at[:, rows(i)] for i in range(4)]
+    targets += [outer_w.at[rows(i)] for i in range(4)]
+    stores = []
+    for i in range(12):
+        loads[i].wait()
+
+        def body(j, carry):
+            part = pl.ds(pl.multiple_of(j * 96, 96), 96)
+            wide[i, part, :] = low[i, part, :].astype(F32)
+            return carry
+
+        lax.fori_loop(0, 8, body, 0)
+        stores.append(pltpu.make_async_copy(wide.at[i], targets[i], out_sem.at[i]))
+        stores[-1].start()
+    singles = (
+        (query_b, QUERY_B), (value_b, VALUE_B), (mixer_b, MIXER_B), (gain_1, GAIN_1),
+        (shift_1, SHIFT_1), (outer_b, OUTER_B), (gain_2, GAIN_2), (shift_2, SHIFT_2),
+    )
+    for ref, row in singles:
+        ref[...] = ext[row : row + 1, :].reshape(MODEL)
+    inner_b[...] = jnp.concatenate([ext[8 + i : 9 + i, :] for i in range(4)], axis=1).reshape(INNER)
+    init[...] = ext[16 : 16 + SLOTS, :]
+    offset[...] = ext[40 : 40 + SLOTS, :]
+    norm[...] = jnp.sqrt(ext[60:61, 0:1] * (1.0 / count))
+    for copy in stores:
+        copy.wait()
+
+
+def widen(packed, ext, chains):
+    square = shape((MODEL, MODEL), F32)
+    line = shape((MODEL,), F32)
+    slots = shape((SLOTS, MODEL), F32)
+    return pl.pallas_call(
+        functools.partial(widen_kernel, chains * SEGS * SLOTS * MODEL),
+        out_shape=(
+            square, square, square, square, shape((MODEL, INNER), F32), shape((INNER, MODEL), F32),
+            line, line, line, line, line, shape((INNER,), F32), line, line, line, slots, slots,
+            shape((1, 1), F32),
+        ),
+        in_specs=[ANY, VMEM],
+        out_specs=(ANY,) * 6 + (VMEM,) * 12,
+        scratch_shapes=[
+            pltpu.VMEM((12, MODEL, MODEL), LOW),
+            pltpu.VMEM((12, MODEL, MODEL), F32),
+            DMA((12,)),
+            DMA((12,)),
+        ],
+        compiler_params=pltpu.CompilerParams(vmem_limit_bytes=60 << 20),
+        name="widen",
+    )(packed, ext)
+
+
 def shards(
     tokens, documents, resets, cotangent, query_weight, query_bias, key_weight, value_weight,
     value_bias, mixer_weight, mixer_bias, first_gain, first_shift, inner_weight, inner_bias,
     outer_weight, outer_bias, second_gain, second_shift, memory_init, write_offset,
 ):
     weights = (query_weight, key_weight, value_weight, mixer_weight, inner_weight, outer_weight)
-    vec = jnp.stack(
-        [
-            query_bias, value_bias, mixer_bias, first_gain, first_shift, outer_bias, second_gain,
-            second_shift,
-        ]
-    ).astype(F32)
-    inner_b = inner_bias.astype(F32)[None]
+    vectors = (
+        query_bias, value_bias, mixer_bias, first_gain, first_shift, outer_bias, second_gain,
+        second_shift,
+    )
     tok = tokens[0]
-    spare = ((0, PAD - SLOTS), (0, 0))
-    init = jnp.pad(memory_init, spare)
-    offset = jnp.pad(write_offset, spare)
-    kv, probs, orow, ow, h1w, zw, h2w, xm = forward(
-        resets, tok, documents[0], init, offset, vec, inner_b, weights
+    kv, probs, orow, ow, h1w, zw, h2w, xm, vec, inner_b = forward(
+        resets, tok, documents[0], memory_init, write_offset, vectors, inner_bias, weights
     )
     layer_output, ub, act, dz, df, da, dh1, dout, sums, inner_sum = middle(
         tok, orow, cotangent[0], vec, inner_b, weights
@@ -1073,36 +1144,14 @@
         ub, act, dz, df, da, weights,
     )
     packed, ext = sum_all(packed, ext)
-    query_w, key_w, value_w, mixer_w = (
-        packed[i * MODEL : (i + 1) * MODEL].astype(F32) for i in range(4)
-    )
-    inner_w = jnp.concatenate(
-        [packed[i * MODEL : (i + 1) * MODEL] for i in range(4, 8)], axis=1
-    ).astype(F32)
-    outer_w = packed[8 * MODEL :].astype(F32)
-    chains = lax.axis_size("chain")
-    memory_norm = jnp.sqrt(ext[60, 0] / (chains * SEGS * SLOTS * MODEL))
+    (
+        query_w, key_w, value_w, mixer_w, inner_w, outer_w, query_b, value_b, mixer_b, gain_1,
+        shift_1, inner_b, outer_b, gain_2, shift_2, init, offset, memory_norm,
+    ) = widen(packed, ext, lax.axis_size("chain"))
     return (
-        layer_output,
-        input_grad,
-        query_w,
-        ext[QUERY_B],
-        key_w,
-        value_w,
-        ext[VALUE_B],
-        mixer_w,
-        ext[MIXER_B],
-        ext[GAIN_1],
-        ext[SHIFT_1],
-        inner_w,
-        ext[8:12].reshape(-1),
-        outer_w,
-        ext[OUTER_B],
-        ext[GAIN_2],
-        ext[SHIFT_2],
-        ext[16:36],
-        ext[40:60],
-        memory_norm,
+        layer_output, input_grad, query_w, query_b, key_w, value_w, value_b, mixer_w, mixer_b,
+        gain_1, shift_1, inner_w, inner_b, outer_w, outer_b, gain_2, shift_2, init, offset,
+        memory_norm.reshape(()),
     )
 
 

time: 290 us -> 268 us (0.924)
  other arithmetic: 18 us -> 0 us
  local copies, waits for them, and re-layouts: 17.2 us -> 1.26 us
  Pallas kernels: 248 us -> 263 us
    pallas_call x0 -> x1, Pallas kernels: none -> 15.2 us  [widen(): pl.pallas_call(functools.partial(widen_kernel, chains * SEGS * SLOTS * MO...]
    convert_element_type x3 -> x0, other arithmetic: 12.9 us -> none  [the longest x1 8.01 us: shards(): outer_w = packed[8 * MODEL:].astype(F32)]
    another operation x9 -> x0, local copies, waits for them, and re-layouts: 5.53 us -> none  [shards(): jnp.stack([query_bias, value_bias, mixer_bias, first_gain, first_shift, o...]
    slice x4 -> x0, local copies, waits for them, and re-layouts: 5.22 us -> none  [the longest x1 1.71 us: shards(): ext[SHIFT_2]]
    slice x1 -> x0, other arithmetic: 3.77 us -> none  [shards(): packed[i * MODEL:(i + 1) * MODEL]]
where the time goes in v2:
time: 268 us; the launch traced here: 266 us
  Pallas kernels  263 us (98%)
    pallas_call x1, Pallas kernels, sum_all(): pl.pallas_call(sum_kernel, out_shape=(jax.ShapeDtypeStruct((2 * HALF, WID...  101 us
    pallas_call x1, Pallas kernels, forward(): pl.pallas_call(forward_kernel, out_shape=(shape((SEGS, KEYS, TRIPLE)), sh...  59.4 us
    pallas_call x1, Pallas kernels, backward(): pl.pallas_call(backward_kernel, out_shape=(shape((4, ROWS, TRIPLE)), shap...  46.8 us
    pallas_call x1, Pallas kernels, middle(): pl.pallas_call(middle_kernel, out_shape=(shape((1, SEGS, BLOCK, MODEL)),...  20.6 us
    pallas_call x1, Pallas kernels, weight_sums(): pl.pallas_call(weight_kernel, out_shape=(shape((12 * MODEL, MODEL)), shap...  20.2 us
    pallas_call x1, Pallas kernels, widen(): pl.pallas_call(functools.partial(widen_kernel, chains * SEGS * SLOTS * MO...  15.2 us

profile of v2, /device:TPU:1, one launch (start us, length us, event | category | flops | bytes accessed | tf_op | source)
XLA Modules:
  0.0 265.6 jit_solution(7773469675419900791)
XLA Ops:
  0.7 1.3 copy.43
  1.9 59.4 %forward_attention.1 = (bf16[3,640,576]{2,1,0:T(8,128)(2,1)}, bf16[3,3,544,640]{3,2,1,0:T(8,128)(2,1)}, bf16[4,384,192]{2,1,0:T(8,128)(2,1)}, bf16[2,4,32,192]{3...) custom-call(s32[1,2]{1,0:T(1,128)} %resets.3, ...), custom_call_target="tpu_custom_call" | custom-call | tf_op jit(solution)/shard_map/forward_attention/pallas_call | solution.py:295
  61.3 20.6 %token_layer.1 = (bf16[1,3,128,768]{3,2,1,0:T(8,128)(2,1)}, bf16[384,768]{1,0:T(8,128)(2,1)}, bf16[384,3072]{1,0:T(8,128)(2,1)}, bf16[384,3072]{1,0:T(8,128)(2,1...) custom-call(bf16[3,128,768]{2,1,0:T(8,128)(2,1)} %bitcast.7, ...), custom_call_target="tpu_custom_call" | custom-call | tf_op jit(solution)/shard_map/token_layer/pallas_call | solution.py:700
  81.9 46.8 %backward_attention.1 = (bf16[4,384,576]{2,1,0:T(8,128)(2,1)}, bf16[3,4,64,576]{3,2,1,0:T(8,128)(2,1)}, bf16[2,32,768]{2,1,0:T(8,128)(2,1)}, bf16[2,32,3072]{2,1...) custom-call(s32[1,2]{1,0:T(1,128)} %resets.3, ...), custom_call_target="tpu_custom_call" | custom-call | tf_op jit(solution)/shard_map/backward_attention/pallas_call | solution.py:912
  128.7 20.2 %weight_sums.1 = (bf16[9216,768]{1,0:T(8,128)(2,1)}, f32[1,3,128,768]{3,2,1,0:T(8,128)}, f32[64,768]{1,0:T(8,128)}) custom-call(bf16[3,128,768]{2,1,0:T(8,128)(2,1)} %bitcast.8, bf16[3,64,768]{2,1,0:T(8,128)(2,1)} %get-tuple-element.75.xm, bf16[4,384,576]{2,1,0:T(8,128)(2,1)} %get-tuple-element.82.drow, bf16[3,4,64,576]{3,2,1,0:T(8,128)(2,1)} %get-tuple-element.83.dmem, ...), custom_call_target="tpu_custom_call" | custom-call | tf_op jit(solution)/shard_map/weight_sums/pallas_call | solution.py:1026
  148.9 101.3 %sum_all.1 = (bf16[9216,768]{1,0:T(8,128)(2,1)}, f32[64,768]{1,0:T(8,128)}) custom-call(bf16[9216,768]{1,0:T(8,128)(2,1)} %get-tuple-element.100.g, f32[64,768]{1,0:T(8,128)} %get-tuple-element.101.ext), custom_call_target="tpu_custom_call" | custom-call | tf_op jit(solution)/shard_map/sum_all/pallas_call | solution.py:606
  250.2 15.2 %widen.1 = (f32[768,768]{1,0:T(8,128)}, f32[768,768]{1,0:T(8,128)}, f32[768,768]{1,0:T(8,128)}, f32[768,768]{1,0:T(8,128)}, f32[768,3072]{1,0:T(8,128)}, /*index...) custom-call(bf16[9216,768]{1,0:T(8,128)(2,1)} %get-tuple-element.102, ...), custom_call_target="tpu_custom_call" | custom-call | tf_op jit(solution)/shard_map/widen/pallas_call | solution.py:1102

commit v3 on v2

--- a/solution.py
+++ b/solution.py
@@ -336,11 +336,10 @@
     )(resets, tok, docs, init, offset, *vectors, inner_b, *weights)
 
 
-WIDE = 768
-HALF = 4608
-PART = 1536
-CHUNK = 384
-SUB = 96
+HALF = 384
+CHUNK = 96
+SUB = 48
+SIDE = 384
 ORDERS = (("x", "y", "z"), ("y", "z", "x"), ("z", "x", "y"))
 
 
@@ -382,251 +381,6 @@
         return carry
 
     lax.fori_loop(0, rows // step, body, 0)
-
-
-def sum_kernel(
-    g, ext, w, e, crecv, r1, r2, r3, r4, ecore, ex, ey, ez,
-    c_s, c_r, a1_s, a1_r, a2_s, a2_r, b_s, b_r, d_s, d_r,
-    gd_s, gd_r, gb_s, gb_r, g1_s, g1_r, g2_s, g2_r, gc_s, gc_r,
-    e_s, e_r,
-):
-    at = places()
-    greet(at, ALL_PEERS)
-    started = []
-
-    def send(src, dst, s_sem, r_sem, axis, off):
-        copy = pltpu.make_async_remote_copy(
-            src_ref=src, dst_ref=dst, send_sem=s_sem, recv_sem=r_sem,
-            device_id=peer(at, axis, off), device_id_type=MESH,
-        )
-        copy.start()
-        started.append(copy)
-        return copy
-
-    core = at["core"]
-    mine = core * HALF
-    theirs = (1 - core) * HALF
-
-    def turn(value, off):
-        return lax.rem(value + off + 4, 4)
-
-    def ds(start, size):
-        return pl.ds(pl.multiple_of(start, 16), size)
-
-    place1 = [at[order[0]] for order in ORDERS]
-    place2 = [at[order[1]] for order in ORDERS]
-    place3 = [at[order[2]] for order in ORDERS]
-
-    def rel(p, off):
-        return p * PART + turn(place1[p], off) * CHUNK
-
-    core_copies = {}
-    e_core = send(
-        ext.at[pl.ds(pl.multiple_of((1 - core) * 32, 8), 32)], ecore, e_s.at[0], e_r.at[0], "core", 1
-    )
-    for j, off in enumerate((2, 1, 3, 0)):
-        for p in range(3):
-            start = rel(p, off)
-            core_copies[p, off] = send(
-                g.at[ds(theirs + start, CHUNK)], crecv.at[ds(start, CHUNK)],
-                c_s.at[p, j], c_r.at[p, j], "core", 1,
-            )
-
-    def own(p, off):
-        core_copies[p, off].wait_recv()
-        start = rel(p, off)
-        add_rows(crecv, start, [(g, mine + start), (crecv, start)], CHUNK)
-
-    e_core.wait_recv()
-    ecore[...] = ext[pl.ds(pl.multiple_of(core * 32, 8), 32), :] + ecore[...]
-    e_x = [
-        send(
-            ecore.at[pl.ds(pl.multiple_of(turn(at["x"], d) * 8, 8), 8)],
-            ex.at[d - 1], e_s.at[d], e_r.at[d], "x", d,
-        )
-        for d in (1, 2, 3)
-    ]
-    first = {}
-    for p in range(3):
-        own(p, 2)
-        start = rel(p, 2)
-        axis = ORDERS[p][0]
-        first[p] = (
-            send(crecv.at[ds(start, CHUNK // 2)], r1.at[p, 0], a1_s.at[p, 0], a1_r.at[p, 0], axis, 1),
-            send(
-                crecv.at[ds(start + CHUNK // 2, CHUNK // 2)], r1.at[p, 1],
-                a1_s.at[p, 1], a1_r.at[p, 1], axis, 3,
-            ),
-        )
-    for off in (1, 3, 0):
-        for p in range(3):
-            own(p, off)
-    second = {}
-    for p in range(3):
-        axis = ORDERS[p][0]
-        start = rel(p, 1)
-        first[p][0].wait_recv()
-        add_rows(crecv, start, [(crecv, start), (r1.at[p, 0], 0)], CHUNK // 2)
-        right = send(crecv.at[ds(start, CHUNK)], r2.at[p, 0], a2_s.at[p, 0], a2_r.at[p, 0], axis, 1)
-        start = rel(p, 3)
-        first[p][1].wait_recv()
-        add_rows(
-            crecv, start + CHUNK // 2, [(crecv, start + CHUNK // 2), (r1.at[p, 1], 0)], CHUNK // 2
-        )
-        left = send(crecv.at[ds(start, CHUNK)], r2.at[p, 1], a2_s.at[p, 1], a2_r.at[p, 1], axis, 3)
-        second[p] = (right, left)
-    e_own = pl.ds(pl.multiple_of(core * 32 + at["x"] * 8, 8), 8)
-    for copy in e_x:
-        copy.wait_recv()
-    ey[pl.ds(at["y"], 1)] = (ecore[pl.ds(pl.multiple_of(at["x"] * 8, 8), 8), :] + ex[0] + ex[1] + ex[2])[None]
-    e_y = [
-        send(ey.at[at["y"]], ey.at[at["y"]], e_s.at[3 + d], e_r.at[3 + d], "y", d)
-        for d in (1, 2, 3)
-    ]
-    third = {}
-    for p in range(3):
-        start = rel(p, 0)
-        for copy in second[p]:
-            copy.wait_recv()
-        add_rows(crecv, start, [(crecv, start), (r2.at[p, 0], 0), (r2.at[p, 1], 0)], CHUNK)
-        third[p] = [
-            send(
-                crecv.at[ds(start + turn(place2[p], d) * SUB, SUB)], r3.at[p, d - 1],
-                b_s.at[p, d - 1], b_r.at[p, d - 1], ORDERS[p][1], d,
-            )
-            for d in (1, 2, 3)
-        ]
-    for copy in e_y:
-        copy.wait_recv()
-    ez[pl.ds(at["z"], 1)] = (ey[0] + ey[1] + ey[2] + ey[3])[None]
-    e_z = [
-        send(ez.at[at["z"]], ez.at[at["z"]], e_s.at[6 + d], e_r.at[6 + d], "z", d)
-        for d in (1, 2, 3)
-    ]
-    fourth = {}
-
-    def quarter(ref, start, c):
-        return ref.at[ds(start + (c // 2) * (SUB // 2), SUB // 2), pl.ds(pl.multiple_of(lax.rem(c, 2) * (WIDE // 2), 128), WIDE // 2)]
-
-    for p in range(3):
-        start = rel(p, 0) + place2[p] * SUB
-        for copy in third[p]:
-            copy.wait_recv()
-        add_rows(crecv, start, [(crecv, start)] + [(r3.at[p, d], 0) for d in range(3)], SUB)
-        fourth[p] = [
-            send(
-                quarter(crecv, start, turn(place3[p], d)), r4.at[p, d - 1],
-                d_s.at[p, d - 1], d_r.at[p, d - 1], ORDERS[p][2], d,
-            )
-            for d in (1, 2, 3)
-        ]
-    for copy in e_z:
-        copy.wait_recv()
-    e[e_own, :] = ez[0] + ez[1] + ez[2] + ez[3]
-    e_back = [
-        send(e.at[e_own], e.at[e_own], e_s.at[9 + d], e_r.at[9 + d], "x", d) for d in (1, 2, 3)
-    ]
-    fifth = {}
-    for p in range(3):
-        start = rel(p, 0) + place2[p] * SUB
-        for copy in fourth[p]:
-            copy.wait_recv()
-        total = quarter(crecv, start, place3[p])[...].astype(jnp.float32)
-        for d in range(3):
-            total = total + r4[p, d].astype(jnp.float32)
-        piece = quarter(w, mine + start, place3[p])
-        piece[...] = total.astype(w.dtype)
-        fifth[p] = [
-            send(piece, piece, gd_s.at[p, d - 1], gd_r.at[p, d - 1], ORDERS[p][2], d)
-            for d in (1, 2, 3)
-        ]
-    sixth = {}
-    for p in range(3):
-        start = mine + rel(p, 0) + place2[p] * SUB
-        for copy in fifth[p]:
-            copy.wait_recv()
-        piece = w.at[ds(start, SUB)]
-        sixth[p] = [
-            send(piece, piece, gb_s.at[p, d - 1], gb_r.at[p, d - 1], ORDERS[p][1], d)
-            for d in (1, 2, 3)
-        ]
-    for copy in e_back:
-        copy.wait_recv()
-    e_half = e.at[pl.ds(pl.multiple_of(core * 32, 8), 32)]
-    e_last = send(e_half, e_half, e_s.at[13], e_r.at[13], "core", 1)
-    seventh = {}
-    last = []
-
-    def across(p, j, start, rows):
-        piece = w.at[ds(start, rows)]
-        last.append(send(piece, piece, gc_s.at[p, j], gc_r.at[p, j], "core", 1))
-
-    for p in range(3):
-        start = mine + rel(p, 0)
-        for copy in sixth[p]:
-            copy.wait_recv()
-        piece = w.at[ds(start, CHUNK)]
-        axis = ORDERS[p][0]
-        seventh[p] = (
-            send(piece, piece, g1_s.at[p, 0], g1_r.at[p, 0], axis, 1),
-            send(piece, piece, g1_s.at[p, 1], g1_r.at[p, 1], axis, 3),
-        )
-        across(p, 0, start, CHUNK)
-    eighth = {}
-    for p in range(3):
-        axis = ORDERS[p][0]
-        seventh[p][0].wait_recv()
-        start = mine + rel(p, 3)
-        piece = w.at[ds(start, CHUNK // 2)]
-        right = send(piece, piece, g2_s.at[p, 0], g2_r.at[p, 0], axis, 1)
-        across(p, 1, start, CHUNK)
-        seventh[p][1].wait_recv()
-        start = mine + rel(p, 1)
-        piece = w.at[ds(start + CHUNK // 2, CHUNK // 2)]
-        left = send(piece, piece, g2_s.at[p, 1], g2_r.at[p, 1], axis, 3)
-        across(p, 2, start, CHUNK)
-        eighth[p] = (right, left)
-    for p in range(3):
-        start = mine + rel(p, 2)
-        for i in range(2):
-            eighth[p][i].wait_recv()
-            across(p, 3 + i, start + i * (CHUNK // 2), CHUNK // 2)
-    e_last.wait_recv()
-    for copy in last:
-        copy.wait_recv()
-    for copy in started:
-        copy.wait_send()
-
-
-def sum_all(g, ext):
-    dma = pltpu.SemaphoreType.DMA
-    pairs = [(3, 4), (3, 2), (3, 2), (3, 3), (3, 3), (3, 3), (3, 3), (3, 2), (3, 2), (3, 5), (14,)]
-    sems = [dma(shape) for shape in pairs for _ in range(2)]
-    vmem = pl.BlockSpec(memory_space=pltpu.VMEM)
-    return pl.pallas_call(
-        sum_kernel,
-        out_shape=(
-            jax.ShapeDtypeStruct((2 * HALF, WIDE), jnp.bfloat16),
-            jax.ShapeDtypeStruct((64, WIDE), jnp.float32),
-        ),
-        in_specs=[vmem, vmem],
-        out_specs=(vmem, vmem),
-        scratch_shapes=[
-            pltpu.VMEM((HALF, WIDE), jnp.bfloat16),
-            pltpu.VMEM((3, 2, CHUNK // 2, WIDE), jnp.bfloat16),
-            pltpu.VMEM((3, 2, CHUNK, WIDE), jnp.bfloat16),
-            pltpu.VMEM((3, 3, SUB, WIDE), jnp.bfloat16),
-            pltpu.VMEM((3, 3, SUB // 2, WIDE // 2), jnp.bfloat16),
-            pltpu.VMEM((32, WIDE), jnp.float32),
-            pltpu.VMEM((3, 8, WIDE), jnp.float32),
-            pltpu.VMEM((4, 8, WIDE), jnp.float32),
-            pltpu.VMEM((4, 8, WIDE), jnp.float32),
-        ] + sems,
-        compiler_params=pltpu.CompilerParams(
-            collective_id=7, has_side_effects=True, vmem_limit_bytes=60 << 20
-        ),
-        name="sum_all",
-    )(g, ext)
 
 
 def middle_kernel(
@@ -731,8 +485,8 @@
 def backward_kernel(
     resets, dout, kv, probs, h1w, zw, h2w, vec,
     wq_h, wk_h, wv_h, wm_h, wi_h, wo_h,
-    drow, dmem, ubw, gw, dzw, dfw, daw, small,
-    wq, wk, wv, wm, wi, wo, doh, dow, ds, acc, dsend, msend, wide,
+    drow, dmem, ubw, gw, dzw, dfw, daw, small, doh, dow, dh1w,
+    wq, wk, wv, wm, wi, wo, acc, dsend, msend, wide,
     w_sem, d_s, d_r, x_s, x_r, m_s, m_r,
 ):
     z = lax.axis_index("seq")
@@ -801,21 +555,21 @@
             msend[s, PAD:, 0:GROUP] = jnp.zeros((PAD, GROUP), LOW)
         msend[s, :, GROUP:] = acc[s, TOKENS : TOKENS + MEMORY, :].astype(LOW)
         mem_copies[s] = [
-            push(started, msend.at[s], dmem.at[s, z], m_s.at[s, d - 1], m_r.at[s, d - 1], d)
+            push(started, msend.at[s], dmem.at[s - 1, z], m_s.at[s, d - 1], m_r.at[s, d - 1], d)
             for d in (1, 2, 3)
         ]
-        dmem[s, z] = msend[s]
+        dmem[s - 1, z] = msend[s]
         dsend[s, :, GROUP:] = acc[s, 0:TOKENS, :].astype(LOW)
-        part = slice(s * BLOCK, (s + 1) * BLOCK)
+        kept = slice((s - 1) * BLOCK, s * BLOCK)
         for d in (1, 2, 3):
             there = pl.ds(pl.multiple_of(ring(d) * BLOCK, BLOCK), BLOCK)
             row_copies.append(
                 push(
-                    started, dsend.at[s, there], drow.at[z, part],
+                    started, dsend.at[s, there], drow.at[z, kept],
                     x_s.at[s, d - 1], x_r.at[s, d - 1], d,
                 )
             )
-        drow[z, part, :] = dsend[s, here, :]
+        drow[z, kept, :] = dsend[s, here, :]
 
     sums = {}
 
@@ -830,7 +584,7 @@
         for g in range(4):
             for t in range(3):
                 wide[t, :, g * GROUP : (g + 1) * GROUP] = dmem[
-                    s, g, :, t * GROUP : (t + 1) * GROUP
+                    s - 1, g, :, t * GROUP : (t + 1) * GROUP
                 ]
         if s == SEGS - 1:
             for copy in fetched:
@@ -842,9 +596,6 @@
         grad = write + d_rows[PAD:]
         add("offset", write)
         add("norm", jnp.sum(jnp.sum(grad * grad, axis=0, keepdims=True), axis=1, keepdims=True))
-        if s == 0:
-            add("init", grad)
-            return None
         flag = jnp.full((PAD, MODEL), resets[0, s - 1], jnp.int32) > 0
         add("init", jnp.where(flag, grad, 0.0))
         return jnp.where(flag, 0.0, grad)
@@ -869,6 +620,8 @@
         add("shift_1", column_sum(d_upper))
         d_first = norm_back(d_upper, unit, inverse, gain_1)
         saved[s] = d_first
+        if s == 0:
+            dh1w[...] = d_first
         d_low = d_first.astype(LOW)
         daw[s] = d_low
         add("mixer", column_sum(d_low))
@@ -881,11 +634,7 @@
     layer_back(1, memory_back(2))
     writes_back(1)
     finish(1)
-    tokens_back(0)
     layer_back(0, memory_back(1))
-    writes_back(0)
-    finish(0)
-    memory_back(0)
     quarter = 0.25
     row = lax.broadcasted_iota(jnp.int32, (24, MODEL), 0)
     zero = jnp.zeros((1, MODEL), F32)
@@ -902,7 +651,7 @@
         sums["offset"][0:24]
         + jnp.where(row >= SLOTS, jnp.broadcast_to(sums["norm"], (24, MODEL)), 0.0)
     )
-    for copy in row_copies:
+    for copy in in_copies[0] + row_copies:
         copy.wait_recv()
     for copy in started:
         copy.wait_send()
@@ -912,22 +661,22 @@
     return pl.pallas_call(
         backward_kernel,
         out_shape=(
-            shape((4, ROWS, TRIPLE)),
-            shape((SEGS, 4, MEMORY, TRIPLE)),
+            shape((4, ROWS - BLOCK, TRIPLE)),
+            shape((SEGS - 1, 4, MEMORY, TRIPLE)),
             shape((2, PAD, MODEL)),
             shape((2, PAD, INNER)),
             shape((2, PAD, INNER)),
             shape((2, PAD, MODEL)),
             shape((2, PAD, MODEL)),
             shape((64, MODEL), F32),
+            shape((SEGS, TOKENS, GROUP)),
+            shape((PAD, GROUP)),
+            shape((PAD, MODEL), F32),
         ),
         in_specs=[pl.BlockSpec(memory_space=pltpu.SMEM)] + [VMEM] * 7 + [ANY] * 6,
-        out_specs=(VMEM,) * 8,
+        out_specs=(VMEM,) * 11,
         scratch_shapes=weight_buffers()
         + [
-            pltpu.VMEM((SEGS, TOKENS, GROUP), LOW),
-            pltpu.VMEM((PAD, GROUP), LOW),
-            pltpu.VMEM((TOKENS, KEYS), LOW),
             pltpu.VMEM((SEGS, KEYS, 2 * GROUP), F32),
             pltpu.VMEM((SEGS, TOKENS, TRIPLE), LOW),
             pltpu.VMEM((SEGS, MEMORY, TRIPLE), LOW),
@@ -949,117 +698,473 @@
 
 FULL = ROWS + MEMORY
 MOST = ROWS + PAD
-
-
-def weight_kernel(
-    tok, xm, drow, dmem, orow, ow, dh1, sums, inner_sum, small, ubw, gw, dzw, dfw, daw,
-    ub_h, act_h, dz_h, df_h, da_h, wq_h, wk_h, wv_h,
+UNITS = ((4, 5, 6), (7, 8, 9), (10, 11, 3), (0, 1, 2))
+
+
+def finish_kernel(
+    tok, xm, drow, dmem, orow, ow, dh1, sums, inner_sum, small, ubw, gw, dzw, dfw, daw, dow, dh1w,
+    kv_h, probs_h, doh_h, ub_h, act_h, dz_h, df_h, da_h, wq_h, wk_h, wv_h,
     packed, input_grad, ext,
-    ub, act, dz, df, da, wq, wk, wv, rows, triple, mixed, w_sem,
+    kv, probs, doh, ub, act, dz, df, da, wq, wk, wv, rows, triple, mixed, acc, dsend, msend,
+    drow0, dmall, wide, g, crecv, r1, r2, r3, slots, own_ext, ecore, ex, ey, ez,
+    w_sem, x_s, x_r, m_s, m_r, c_s, c_r, a_s, a_r, b_s, b_r, d_s, d_r, e_s, e_r, f_s, f_r,
+    loc, free, n_s, n_r, o_s, o_r, gc_s, gc_r, t_s, t_r,
 ):
-    z = lax.axis_index("seq")
+    at = places()
+    z = at["z"]
+    core = at["core"]
     top = pl.ds(0, ROWS)
     fetched = fetch(
         [
-            (wq_h, wq), (wk_h, wk), (wv_h, wv), (da_h, da.at[top]), (ub_h, ub.at[top]),
-            (dz_h, dz.at[top]), (df_h, df.at[top]), (act_h, act.at[top]),
+            (ub_h, ub.at[top]), (dz_h, dz.at[top]), (kv_h.at[0], kv), (probs_h.at[0], probs),
+            (doh_h.at[0], doh), (act_h, act.at[top]), (df_h, df.at[top]), (da_h, da.at[top]),
+            (wq_h, wq), (wk_h, wk), (wv_h, wv),
         ],
         w_sem,
     )
-    at = jnp.minimum(z, 2)
-    keep = (z < SEGS).astype(F32).astype(LOW)
+    started = []
+
+    def send(src, dst, s_sem, r_sem, axis, off):
+        copy = pltpu.make_async_remote_copy(
+            src_ref=src, dst_ref=dst, send_sem=s_sem, recv_sem=r_sem,
+            device_id=peer(at, axis, off), device_id_type=MESH,
+        )
+        copy.start()
+        started.append(copy)
+        return copy
+
+    def turn(value, off):
+        return lax.rem(value + off + 4, 4)
+
+    def ds(start, size):
+        return pl.ds(pl.multiple_of(start, 16), size)
+
+    place1 = [at[order[0]] for order in ORDERS]
+    place2 = [at[order[1]] for order in ORDERS]
+    place3 = [at[order[2]] for order in ORDERS]
+    live = {}
+
+    def sub_of(ref, start, n):
+        side = pl.ds(pl.multiple_of(lax.rem(n, 2) * SIDE, 128), SIDE)
+        return ref.at[ds(start + (n // 2) * SUB, SUB), side]
+
+    def home(p, off):
+        return core * HALF + turn(place1[p], off) * CHUNK
+
+    def block_done(u, p):
+        b = UNITS[u][p]
+        live["core", u, p] = send(
+            g.at[b, ds((1 - core) * HALF, HALF)], crecv.at[u, p],
+            c_s.at[u, p], c_r.at[u, p], "core", 1,
+        )
+        started.pop()
+
+    def stage1(u):
+        for p in range(3):
+            b = UNITS[u][p]
+            live["core", u, p].wait_recv()
+            held = crecv.at[u, p]
+            start = turn(place1[p], 2) * CHUNK
+            add_rows(held, start, [(g.at[b], core * HALF + start), (held, start)], CHUNK)
+            live["a", u, p] = [
+                send(
+                    held.at[ds(start + i * SUB, SUB)], r1.at[u, p, i],
+                    a_s.at[u, p, i], a_r.at[u, p, i], ORDERS[p][0], 1 + 2 * i,
+                )
+                for i in range(2)
+            ]
+        for p in range(3):
+            b = UNITS[u][p]
+            held = crecv.at[u, p]
+            for off in (1, 3, 0):
+                start = turn(place1[p], off) * CHUNK
+                add_rows(held, start, [(g.at[b], core * HALF + start), (held, start)], CHUNK)
+            live["core", u, p].wait_send()
+        pl.semaphore_signal(
+            free.at[u], inc=1, device_id=peer(at, "core", 1), device_id_type=MESH
+        )
+
+    def stage2(u):
+        for p in range(3):
+            held = crecv.at[u, p]
+            live["b", u, p] = []
+            for i in range(2):
+                start = turn(place1[p], 1 + 2 * i) * CHUNK
+                live["a", u, p][i].wait_recv()
+                half = start + i * SUB
+                add_rows(held, half, [(held, half), (r1.at[u, p, i], 0)], SUB)
+                live["b", u, p].append(
+                    send(
+                        held.at[ds(start, CHUNK)], r2.at[u, p, i],
+                        b_s.at[u, p, i], b_r.at[u, p, i], ORDERS[p][0], 1 + 2 * i,
+                    )
+                )
+
+    def stage3(u):
+        for p in range(3):
+            held = crecv.at[u, p]
+            start = place1[p] * CHUNK
+            for copy in live["b", u, p]:
+                copy.wait_recv()
+            add_rows(held, start, [(held, start), (r2.at[u, p, 0], 0), (r2.at[u, p, 1], 0)], CHUNK)
+            live["d", u, p] = [
+                send(
+                    sub_of(held, start, turn(place2[p], d)), r3.at[u, p, d - 1],
+                    d_s.at[u, p, d - 1], d_r.at[u, p, d - 1], ORDERS[p][1], d,
+                )
+                for d in (1, 2, 3)
+            ]
+
+    def stage4(u):
+        for p in range(3):
+            for copy in live["d", u, p]:
+                copy.wait_recv()
+            total = sub_of(crecv.at[u, p], place1[p] * CHUNK, place2[p])[...].astype(F32)
+            for d in range(3):
+                total = total + r3[u, p, d].astype(F32)
+            slots[u, p, pl.ds(place3[p], 1)] = total.astype(LOW)[None]
+            live["e", u, p] = [
+                send(
+                    slots.at[u, p, place3[p]], slots.at[u, p, place3[p]],
+                    e_s.at[u, p, d - 1], e_r.at[u, p, d - 1], ORDERS[p][2], d,
+                )
+                for d in (1, 2, 3)
+            ]
+
+    def stage5(u):
+        for p in range(3):
+            for copy in live["e", u, p]:
+                copy.wait_recv()
+            total = slots[u, p, 0].astype(F32)
+            for i in range(1, 4):
+                total = total + slots[u, p, i].astype(F32)
+            target = sub_of(g.at[UNITS[u][p]], home(p, 0), place2[p])
+            target[...] = total.astype(LOW)
+            live["f", u, p] = [
+                send(target, target, f_s.at[u, p, d - 1], f_r.at[u, p, d - 1], ORDERS[p][1], d)
+                for d in (1, 2, 3)
+            ]
+
+    def across(u, p, j, start, count):
+        piece = g.at[UNITS[u][p], ds(start, count)]
+        live["gc", u, p, j] = send(piece, piece, gc_s.at[u, p, j], gc_r.at[u, p, j], "core", 1)
+
+    def stage6(u):
+        pl.semaphore_wait(free.at[u], 1)
+        for p in range(3):
+            for copy in live["f", u, p]:
+                copy.wait_recv()
+            piece = g.at[UNITS[u][p], ds(home(p, 0), CHUNK)]
+            live["n", u, p] = [
+                send(piece, piece, n_s.at[u, p, i], n_r.at[u, p, i], ORDERS[p][0], 1 + 2 * i)
+                for i in range(2)
+            ]
+            across(u, p, 0, home(p, 0), CHUNK)
+
+    def stage7(u):
+        for p in range(3):
+            live["o", u, p] = []
+            for i in range(2):
+                live["n", u, p][i].wait_recv()
+                start = home(p, 3 - 2 * i)
+                piece = g.at[UNITS[u][p], ds(start + i * SUB, SUB)]
+                live["o", u, p].append(
+                    send(piece, piece, o_s.at[u, p, i], o_r.at[u, p, i], ORDERS[p][0], 1 + 2 * i)
+                )
+                across(u, p, 1 + i, start, CHUNK)
+
+    def stage8(u):
+        for p in range(3):
+            for i in range(2):
+                live["o", u, p][i].wait_recv()
+                across(u, p, 3 + i, home(p, 2) + i * SUB, SUB)
+
+    stores = []
+
+    def stage9(u):
+        for p in range(3):
+            for j in range(5):
+                live["gc", u, p, j].wait_recv()
+            b = UNITS[u][p]
+            stores.append(
+                pltpu.make_async_copy(
+                    g.at[b], packed.at[pl.ds(b * MODEL, MODEL)], loc.at[u, p]
+                )
+            )
+            stores[-1].start()
+
+    stages = {
+        1: stage1, 2: stage2, 3: stage3, 4: stage4, 5: stage5, 6: stage6, 7: stage7, 8: stage8,
+        9: stage9,
+    }
+
+    def wave(*pairs):
+        for u, k in pairs:
+            stages[k](u)
+
     low_at = jnp.minimum(z, 1)
     low_keep = (z < 2).astype(F32).astype(LOW)
-    rows[0:ROWS, :] = tok[...].reshape(ROWS, MODEL)
-    rows[ROWS:, :] = xm[at]
-    for g in range(4):
-        for t in range(3):
-            cut = slice(g * GROUP, (g + 1) * GROUP)
-            part = slice(t * GROUP, (t + 1) * GROUP)
-            triple[t, 0:ROWS, cut] = drow[g, :, part]
-            triple[t, ROWS:, cut] = dmem[at, g, :, part] * keep
-        mixed[g, 0:ROWS, :] = orow[g]
-        mixed[g, ROWS:, :] = ow[low_at, g]
+    at_seg = jnp.minimum(z, 2)
+    keep = (z < SEGS).astype(F32).astype(LOW)
+
+    def inner_block(j):
+        g[4 + j] = t_dot(ub[...], dz[:, j * MODEL : (j + 1) * MODEL]).astype(LOW)
+
+    def outer_block(j):
+        g[8 + j] = t_dot(act[:, j * MODEL : (j + 1) * MODEL], df[...]).astype(LOW)
+
+    def mixer_block():
+        for i in range(4):
+            mixed[i, 0:ROWS, :] = orow[i]
+            mixed[i, ROWS:, :] = ow[low_at, i]
+        for i in range(4):
+            g[3, i * GROUP : (i + 1) * GROUP, :] = t_dot(mixed[i], da[...]).astype(LOW)
+
+    def head_back(h, d_rows, part):
+        cut = slice(h * HEAD, (h + 1) * HEAD)
+        key_head = kv[:, GROUP + h * HEAD : GROUP + (h + 1) * HEAD]
+        value_head = kv[:, 2 * GROUP + h * HEAD : 2 * GROUP + (h + 1) * HEAD]
+        d_head = d_rows[:, cut]
+        prob = probs[h, part, :]
+        wide_prob = prob.astype(F32)
+        product = wide_prob * dot_t(d_head, value_head)
+        delta = jnp.sum(product, axis=-1, keepdims=True)
+        d_scores = (product - wide_prob * delta).astype(LOW)
+        d_query = (dot(d_scores, key_head) * SCALE).astype(LOW)
+        return d_query, t_dot(d_scores, kv[part, cut]), t_dot(prob, d_head)
+
+    def head_tokens(h):
+        cut = slice(h * HEAD, (h + 1) * HEAD)
+        d_query, d_key, d_value = head_back(h, doh[...], slice(0, TOKENS))
+        dsend[:, cut] = d_query
+        acc[:, cut] = d_key
+        acc[:, GROUP + h * HEAD : GROUP + (h + 1) * HEAD] = d_value
+
+    def head_writes(h):
+        cut = slice(h * HEAD, (h + 1) * HEAD)
+        d_query, d_key, d_value = head_back(h, dow[...], slice(TOKENS, TOKENS + PAD))
+        msend[0:PAD, cut] = d_query
+        acc[:, cut] += d_key
+        acc[:, GROUP + h * HEAD : GROUP + (h + 1) * HEAD] += d_value
+
+    greet(at, ALL_PEERS)
     ub[ROWS:, :] = ubw[low_at]
     act[ROWS:, :] = gw[low_at]
     dz[ROWS:, :] = dzw[low_at] * low_keep
     df[ROWS:, :] = dfw[low_at] * low_keep
     da[ROWS:, :] = daw[low_at] * low_keep
-    ext[...] = small[...]
-    ext[0:8, :] += sums[...]
-    ext[8:12, :] += jnp.concatenate(
-        [inner_sum[:, i * MODEL : (i + 1) * MODEL] for i in range(4)], axis=0
-    )
-    ext[QUERY_B : QUERY_B + 1, :] += column_sum(triple[0])
-    ext[VALUE_B : VALUE_B + 1, :] += column_sum(triple[2])
+    for copy in fetched[:2]:
+        copy.wait()
+    for j in range(3):
+        inner_block(j)
+        block_done(0, j)
+    for copy in fetched[2:5]:
+        copy.wait()
+    head_tokens(0)
+    wave((0, 1))
+    head_tokens(1)
+    head_tokens(2)
+    for h in range(MINE):
+        head_writes(h)
+    msend[PAD:, 0:GROUP] = jnp.zeros((PAD, GROUP), LOW)
+    msend[:, GROUP:] = acc[TOKENS : TOKENS + MEMORY, :].astype(LOW)
+    dsend[:, GROUP:] = acc[0:TOKENS, :].astype(LOW)
+    row_copies = []
+    for d in (1, 2, 3):
+        there = ds(ring(d) * BLOCK, BLOCK)
+        row_copies.append(
+            send(dsend.at[there], drow0.at[z], x_s.at[d - 1], x_r.at[d - 1], "z", d)
+        )
+        row_copies.append(
+            send(msend, dmall.at[0, z], m_s.at[d - 1], m_r.at[d - 1], "z", d)
+        )
+    drow0[z] = dsend[ds(z * BLOCK, BLOCK), :]
+    dmall[0, z] = msend[...]
+    dmall[1:] = dmem[...]
+    wave((0, 2))
+    inner_block(3)
+    block_done(1, 0)
+    for copy in fetched[5:7]:
+        copy.wait()
+    for j in range(2):
+        outer_block(j)
+        block_done(1, 1 + j)
+    wave((0, 3), (1, 1))
+    for j in range(2, 4):
+        outer_block(j)
+        block_done(2, j - 2)
+    fetched[7].wait()
+    mixer_block()
+    block_done(2, 2)
+    wave((0, 4), (1, 2), (2, 1))
+    rows[0:ROWS, :] = tok[...].reshape(ROWS, MODEL)
+    rows[ROWS:, :] = xm[at_seg]
+    for copy in row_copies:
+        copy.wait_recv()
+    for i in range(4):
+        for t in range(3):
+            cut = slice(i * GROUP, (i + 1) * GROUP)
+            part = slice(t * GROUP, (t + 1) * GROUP)
+            triple[t, 0:BLOCK, cut] = drow0[i, :, part]
+            triple[t, BLOCK:ROWS, cut] = drow[i, :, part]
+            triple[t, ROWS:, cut] = dmall[at_seg, i, :, part] * keep
+            wide[t, :, cut] = dmall[0, i, :, part]
     for t in range(3):
-        packed[t * MODEL : (t + 1) * MODEL, :] = t_dot(rows[...], triple[t]).astype(LOW)
-    for copy in fetched[:4]:
+        g[t] = t_dot(rows[...], triple[t]).astype(LOW)
+        block_done(3, t)
+    wave((0, 5), (1, 3), (2, 2), (3, 1))
+    for copy in fetched[8:]:
         copy.wait()
-    for g in range(4):
-        start = 3 * MODEL + g * GROUP
-        packed[start : start + GROUP, :] = t_dot(mixed[g], da[...]).astype(LOW)
+    d_rows = dot_t(wide[0], wq[...]) + dot_t(wide[1], wk[...]) + dot_t(wide[2], wv[...])
+    write = d_rows[0:PAD] + dh1w[...]
+    grad = write + d_rows[PAD:]
+    norm = jnp.sum(jnp.sum(grad * grad, axis=0, keepdims=True), axis=1, keepdims=True)
+    own_ext[0:8, :] = small[0:8, :] + sums[...]
+    own_ext[8:16, :] = small[8:16, :] + jnp.concatenate(
+        [inner_sum[:, i * MODEL : (i + 1) * MODEL] for i in range(4)]
+        + [jnp.zeros((4, MODEL), F32)],
+        axis=0,
+    )
+    own_ext[QUERY_B : QUERY_B + 1, :] += column_sum(triple[0])
+    own_ext[VALUE_B : VALUE_B + 1, :] += column_sum(triple[2])
+    row = lax.broadcasted_iota(jnp.int32, (24, MODEL), 0)
+    own_ext[16:40, :] = small[16:40, :] + 0.25 * grad[0:24]
+    own_ext[40:64, :] = small[40:64, :] + 0.25 * (
+        write[0:24] + jnp.where(row >= SLOTS, jnp.broadcast_to(norm, (24, MODEL)), 0.0)
+    )
+    half = pl.ds(pl.multiple_of(core * 32, 8), 32)
+    other = pl.ds(pl.multiple_of((1 - core) * 32, 8), 32)
+    small_core = send(own_ext.at[other], ecore, t_s.at[0], t_r.at[0], "core", 1)
+    wave((0, 6), (1, 4), (2, 3), (3, 2))
+    small_core.wait_recv()
+    ecore[...] = own_ext[half, :] + ecore[...]
+    small_x = [
+        send(
+            ecore.at[pl.ds(pl.multiple_of(turn(at["x"], d) * 8, 8), 8)],
+            ex.at[d - 1], t_s.at[d], t_r.at[d], "x", d,
+        )
+        for d in (1, 2, 3)
+    ]
     input_grad[...] = (
         dh1[...]
         + dot_t(triple[0, 0:ROWS, :], wq[...])
         + dot_t(triple[1, 0:ROWS, :], wk[...])
         + dot_t(triple[2, 0:ROWS, :], wv[...])
     ).reshape(1, SEGS, BLOCK, MODEL)
-    for copy in fetched[4:]:
+    wave((0, 7), (1, 5), (2, 4), (3, 3))
+    for copy in small_x:
+        copy.wait_recv()
+    ey[pl.ds(at["y"], 1)] = (
+        ecore[pl.ds(pl.multiple_of(at["x"] * 8, 8), 8), :] + ex[0] + ex[1] + ex[2]
+    )[None]
+    small_y = [
+        send(ey.at[at["y"]], ey.at[at["y"]], t_s.at[3 + d], t_r.at[3 + d], "y", d)
+        for d in (1, 2, 3)
+    ]
+    wave((0, 8), (1, 6), (2, 5), (3, 4))
+    for copy in small_y:
+        copy.wait_recv()
+    ez[pl.ds(at["z"], 1)] = (ey[0] + ey[1] + ey[2] + ey[3])[None]
+    small_z = [
+        send(ez.at[at["z"]], ez.at[at["z"]], t_s.at[6 + d], t_r.at[6 + d], "z", d)
+        for d in (1, 2, 3)
+    ]
+    wave((1, 7), (2, 6), (3, 5))
+    for copy in small_z:
+        copy.wait_recv()
+    mine = pl.ds(pl.multiple_of(core * 32 + at["x"] * 8, 8), 8)
+    ext[mine, :] = ez[0] + ez[1] + ez[2] + ez[3]
+    small_back = [
+        send(ext.at[mine], ext.at[mine], t_s.at[9 + d], t_r.at[9 + d], "x", d) for d in (1, 2, 3)
+    ]
+    wave((1, 8), (2, 7), (3, 6), (0, 9))
+    for copy in small_back:
+        copy.wait_recv()
+    small_last = send(ext.at[half], ext.at[half], t_s.at[13], t_r.at[13], "core", 1)
+    wave((2, 8), (3, 7), (1, 9), (3, 8), (2, 9))
+    small_last.wait_recv()
+    wave((3, 9))
+    for copy in started:
+        copy.wait_send()
+    for copy in stores:
         copy.wait()
 
-    def inner(j, carry):
-        cut = pl.ds(pl.multiple_of(j * MODEL, MODEL), MODEL)
-        there = pl.ds(pl.multiple_of((4 + j) * MODEL, MODEL), MODEL)
-        packed[there, :] = t_dot(ub[...], dz[:, cut]).astype(LOW)
-        there = pl.ds(pl.multiple_of((8 + j) * MODEL, MODEL), MODEL)
-        packed[there, :] = t_dot(act[:, cut], df[...]).astype(LOW)
-        return carry
-
-    lax.fori_loop(0, 4, inner, 0)
-
-
-def weight_sums(
-    tok, xm, drow, dmem, orow, ow, dh1, sums, inner_sum, small, ubw, gw, dzw, dfw, daw,
-    ub, act, dz, df, da, weights,
-):
+
+def finish_all(near, far):
+    def buffer(*dims):
+        return pltpu.VMEM(dims, LOW)
+
+    def wide_buffer(*dims):
+        return pltpu.VMEM(dims, F32)
+
+    pairs = [
+        (3,), (3,), (4, 3), (4, 3, 2), (4, 3, 2), (4, 3, 3), (4, 3, 3), (4, 3, 3), None,
+        (4, 3, 2), (4, 3, 2), (4, 3, 5), (14,),
+    ]
+    sems = [DMA((11,))]
+    for dims in pairs:
+        if dims is None:
+            sems += [DMA((4, 3)), pltpu.SemaphoreType.REGULAR((4,))]
+        else:
+            sems += [DMA(dims), DMA(dims)]
     return pl.pallas_call(
-        weight_kernel,
+        finish_kernel,
         out_shape=(
             shape((12 * MODEL, MODEL)),
             shape((1, SEGS, BLOCK, MODEL), F32),
             shape((64, MODEL), F32),
         ),
-        in_specs=[VMEM] * 15 + [ANY] * 8,
-        out_specs=(VMEM,) * 3,
+        in_specs=[VMEM] * len(near) + [ANY] * len(far),
+        out_specs=(ANY, VMEM, VMEM),
         scratch_shapes=[
-            pltpu.VMEM((MOST, MODEL), LOW),
-            pltpu.VMEM((MOST, INNER), LOW),
-            pltpu.VMEM((MOST, INNER), LOW),
-            pltpu.VMEM((MOST, MODEL), LOW),
-            pltpu.VMEM((MOST, MODEL), LOW),
-            pltpu.VMEM((MODEL, MODEL), LOW),
-            pltpu.VMEM((MODEL, MODEL), LOW),
-            pltpu.VMEM((MODEL, MODEL), LOW),
-            pltpu.VMEM((FULL, MODEL), LOW),
-            pltpu.VMEM((3, FULL, MODEL), LOW),
-            pltpu.VMEM((4, MOST, GROUP), LOW),
-            DMA((8,)),
-        ],
-        compiler_params=pltpu.CompilerParams(vmem_limit_bytes=60 << 20),
-        name="weight_sums",
-    )(
-        tok, xm, drow, dmem, orow, ow, dh1, sums, inner_sum, small, ubw, gw, dzw, dfw, daw,
-        ub, act, dz, df, da, *weights[:3],
-    )
+            buffer(KEYS, TRIPLE),
+            buffer(MINE, QUERIES, KEYS),
+            buffer(TOKENS, GROUP),
+            buffer(MOST, MODEL),
+            buffer(MOST, INNER),
+            buffer(MOST, INNER),
+            buffer(MOST, MODEL),
+            buffer(MOST, MODEL),
+            buffer(MODEL, MODEL),
+            buffer(MODEL, MODEL),
+            buffer(MODEL, MODEL),
+            buffer(FULL, MODEL),
+            buffer(3, FULL, MODEL),
+            buffer(4, MOST, GROUP),
+            wide_buffer(KEYS, 2 * GROUP),
+            buffer(TOKENS, TRIPLE),
+            buffer(MEMORY, TRIPLE),
+            buffer(4, BLOCK, TRIPLE),
+            buffer(SEGS, 4, MEMORY, TRIPLE),
+            buffer(3, MEMORY, MODEL),
+            buffer(12, MODEL, MODEL),
+            buffer(4, 3, HALF, MODEL),
+            buffer(4, 3, 2, SUB, MODEL),
+            buffer(4, 3, 2, CHUNK, MODEL),
+            buffer(4, 3, 3, SUB, SIDE),
+            buffer(4, 3, 4, SUB, SIDE),
+            wide_buffer(64, MODEL),
+            wide_buffer(32, MODEL),
+            wide_buffer(3, 8, MODEL),
+            wide_buffer(4, 8, MODEL),
+            wide_buffer(4, 8, MODEL),
+        ]
+        + sems,
+        compiler_params=pltpu.CompilerParams(
+            collective_id=3, has_side_effects=True, vmem_limit_bytes=62 << 20
+        ),
+        name="weights_and_sums",
+    )(*near, *far)
 
 
 def widen_kernel(
-    count, packed, ext,
-    query_w, key_w, value_w, mixer_w, inner_w, outer_w, query_b, value_b, mixer_b, gain_1, shift_1,
+    count, packed, ext, grad_in,
+    grad_out, query_w, key_w, value_w, mixer_w, inner_w, outer_w, query_b, value_b, mixer_b, gain_1, shift_1,
     inner_b, outer_b, gain_2, shift_2, init, offset, norm,
     low, wide, in_sem, out_sem,
 ):
+    through = pltpu.make_async_copy(grad_in, grad_out, in_sem.at[12])
+    through.start()
     def rows(i):
         return pl.ds(i * MODEL, MODEL)
 
@@ -1093,30 +1198,31 @@
     norm[...] = jnp.sqrt(ext[60:61, 0:1] * (1.0 / count))
     for copy in stores:
         copy.wait()
-
-
-def widen(packed, ext, chains):
+    through.wait()
+
+
+def widen(packed, ext, input_grad, chains):
     square = shape((MODEL, MODEL), F32)
     line = shape((MODEL,), F32)
     slots = shape((SLOTS, MODEL), F32)
     return pl.pallas_call(
         functools.partial(widen_kernel, chains * SEGS * SLOTS * MODEL),
         out_shape=(
-            square, square, square, square, shape((MODEL, INNER), F32), shape((INNER, MODEL), F32),
+            shape((1, SEGS, BLOCK, MODEL), F32), square, square, square, square, shape((MODEL, INNER), F32), shape((INNER, MODEL), F32),
             line, line, line, line, line, shape((INNER,), F32), line, line, line, slots, slots,
             shape((1, 1), F32),
         ),
-        in_specs=[ANY, VMEM],
-        out_specs=(ANY,) * 6 + (VMEM,) * 12,
+        in_specs=[ANY, VMEM, VMEM],
+        out_specs=(ANY,) * 7 + (VMEM,) * 12,
         scratch_shapes=[
             pltpu.VMEM((12, MODEL, MODEL), LOW),
             pltpu.VMEM((12, MODEL, MODEL), F32),
-            DMA((12,)),
+            DMA((13,)),
             DMA((12,)),
         ],
         compiler_params=pltpu.CompilerParams(vmem_limit_bytes=60 << 20),
         name="widen",
-    )(packed, ext)
+    )(packed, ext, input_grad)
 
 
 def shards(
@@ -1136,18 +1242,20 @@
     layer_output, ub, act, dz, df, da, dh1, dout, sums, inner_sum = middle(
         tok, orow, cotangent[0], vec, inner_b, weights
     )
-    drow, dmem, ubw, gw, dzw, dfw, daw, small = backward(
+    drow, dmem, ubw, gw, dzw, dfw, daw, small, doh, dow, dh1w = backward(
         resets, dout, kv, probs, h1w, zw, h2w, vec, weights
     )
-    packed, input_grad, ext = weight_sums(
-        tok, xm, drow, dmem, orow, ow, dh1, sums, inner_sum, small, ubw, gw, dzw, dfw, daw,
-        ub, act, dz, df, da, weights,
-    )
-    packed, ext = sum_all(packed, ext)
+    packed, input_grad, ext = finish_all(
+        (
+            tok, xm, drow, dmem, orow, ow, dh1, sums, inner_sum, small, ubw, gw, dzw, dfw, daw,
+            dow, dh1w,
+        ),
+        (kv, probs, doh, ub, act, dz, df, da) + weights[:3],
+    )
     (
-        query_w, key_w, value_w, mixer_w, inner_w, outer_w, query_b, value_b, mixer_b, gain_1,
+        input_grad, query_w, key_w, value_w, mixer_w, inner_w, outer_w, query_b, value_b, mixer_b, gain_1,
         shift_1, inner_b, outer_b, gain_2, shift_2, init, offset, memory_norm,
-    ) = widen(packed, ext, lax.axis_size("chain"))
+    ) = widen(packed, ext, input_grad, lax.axis_size("chain"))
     return (
         layer_output, input_grad, query_w, query_b, key_w, value_w, value_b, mixer_w, mixer_b,
         gain_1, shift_1, inner_w, inner_b, outer_w, outer_b, gain_2, shift_2, init, offset,

time: 268 us -> 247 us (0.922)
  Pallas kernels: 263 us -> 242 us
    pallas_call x3 -> x2, Pallas kernels: 168 us -> 146 us  [the longest x1 108 us: finish_all(): pl.pallas_call(finish_kernel, out_shape=(shape((12 * MODEL, MODEL)), shap...]
where the time goes in v3:
time: 247 us; the launch traced here: 244 us
  Pallas kernels  242 us (98%)
    pallas_call x1, Pallas kernels, finish_all(): pl.pallas_call(finish_kernel, out_shape=(shape((12 * MODEL, MODEL)), shap...  108 us
    pallas_call x1, Pallas kernels, forward(): pl.pallas_call(forward_kernel, out_shape=(shape((SEGS, KEYS, TRIPLE)), sh...  59.5 us
    pallas_call x1, Pallas kernels, backward(): pl.pallas_call(backward_kernel, out_shape=(shape((4, ROWS - BLOCK, TRIPLE...  37.4 us
    pallas_call x1, Pallas kernels, middle(): pl.pallas_call(middle_kernel, out_shape=(shape((1, SEGS, BLOCK, MODEL)),...  20.5 us
    pallas_call x1, Pallas kernels, widen(): pl.pallas_call(functools.partial(widen_kernel, chains * SEGS * SLOTS * MO...  16.1 us

profile of v3, /device:TPU:1, one launch (start us, length us, event | category | flops | bytes accessed | tf_op | source)
XLA Modules:
  0.0 244.0 jit_solution(13888598366669188814)
XLA Ops:
  0.7 1.3 copy.43
  1.9 59.5 %forward_attention.1 = (bf16[3,640,576]{2,1,0:T(8,128)(2,1)}, bf16[3,3,544,640]{3,2,1,0:T(8,128)(2,1)}, bf16[4,384,192]{2,1,0:T(8,128)(2,1)}, bf16[2,4,32,192]{3...) custom-call(s32[1,2]{1,0:T(1,128)} %resets.3, ...), custom_call_target="tpu_custom_call" | custom-call | tf_op jit(solution)/shard_map/forward_attention/pallas_call | solution.py:295
  61.4 20.5 %token_layer.1 = (bf16[1,3,128,768]{3,2,1,0:T(8,128)(2,1)}, bf16[384,768]{1,0:T(8,128)(2,1)}, bf16[384,3072]{1,0:T(8,128)(2,1)}, bf16[384,3072]{1,0:T(8,128)(2,1...) custom-call(bf16[3,128,768]{2,1,0:T(8,128)(2,1)} %bitcast.7, ...), custom_call_target="tpu_custom_call" | custom-call | tf_op jit(solution)/shard_map/token_layer/pallas_call | solution.py:454
  81.9 37.4 %backward_attention.1 = (bf16[4,256,576]{2,1,0:T(8,128)(2,1)}, bf16[2,4,64,576]{3,2,1,0:T(8,128)(2,1)}, bf16[2,32,768]{2,1,0:T(8,128)(2,1)}, bf16[2,32,3072]{2,1...) custom-call(s32[1,2]{1,0:T(1,128)} %resets.3, ...), custom_call_target="tpu_custom_call" | custom-call | tf_op jit(solution)/shard_map/backward_attention/pallas_call | solution.py:661
  119.4 108.3 %weights_and_sums.1 = (bf16[9216,768]{1,0:T(8,128)(2,1)}, f32[1,3,128,768]{3,2,1,0:T(8,128)}, f32[64,768]{1,0:T(8,128)}) custom-call(bf16[3,128,768]{2,1,0:T(8,128)(2,1)} %bitcast.8, bf16[3,64,768]{2,1,0:T(8,128)(2,1)} %get-tuple-element.77.xm, bf16[4,256,576]{2,1,0:T(8,128)(2,1)} %get-tuple-element.84.drow, bf16[2,4,64,576]{3,2,1,0:T(8,128)(2,1)} %get-tuple-element.85.dmem, ...), custom_call_target="tpu_custom_call" | custom-call | tf_op jit(solution)/shard_map/weights_and_sums/pallas_call | solution.py:1110
  227.7 16.1 %widen.1 = (f32[1,3,128,768]{3,2,1,0:T(8,128)}, f32[768,768]{1,0:T(8,128)}, f32[768,768]{1,0:T(8,128)}, f32[768,768]{1,0:T(8,128)}, f32[768,768]{1,0:T(8,128)}, ...) custom-call(bf16[9216,768]{1,0:T(8,128)(2,1)} %get-tuple-element.104, ...), custom_call_target="tpu_custom_call" | custom-call | tf_op jit(solution)/shard_map/widen/pallas_call | solution.py:1208
